TPU v7x, 32 devices: a whole 2x2x4 slice. The times are simulated.
32 devices in a mesh: pole: 1, prow: 8 (over y, x, core), pcol: 4 (over z).
Axes of the slice: x: 2, y: 2, z: 4, core: 2. Of those that a mesh axis runs over, the one named last changes fastest.
Arguments:
- hamiltonian: bfloat16 [6144, 6144], P(('prow', 'pcol')), may hold values from -2 to 32, as said below
- margin: bfloat16 [6144, 6144], P(('prow', 'pcol')), may hold values from -1 to 1, as said below
- pole_shift: float32 [2], P('pole'), may hold values from 0.3 to 1.5
- row_map: int32 [6144], P('prow'), may hold values from 0 to 6143, as said below
- parent: int32 [48], replicated, may hold values from 1 to 48, as said below
Outputs:
- factored: float32 [2, 6144, 6144], P('pole', 'prow', 'pcol')
Inputs may be any that keep to these rules, and one draw needn't show every extreme that they name: For each aligned block of 768 rows, row_map maps the block's rows one to one onto the same block's indices. parent[s] is greater than s; the value 48 marks a root. Supernode 0's parent is 1 and the last supernode is a root. `hamiltonian`: as a matrix over orbitals it is symmetric. `margin`: as a matrix over orbitals it is symmetric, with ones on its diagonal.
All inputs are finite; a program needn't handle non-finite values.
Results may differ from a plain program's by a relative error of at most 0.0023.
Values may be sent and summed in bfloat16 or wider, within the bound.
A program may use at most 128 MiB of HBM per device.

v0:
```python
import jax
import jax.numpy as jnp
from jax import lax
from jax.sharding import PartitionSpec as P

SN = 128
STEPS = 3
NSI = 4


def broadcast(array, axis, root):
    mine = lax.axis_index(axis) == root
    return lax.psum(jnp.where(mine, array, jnp.zeros_like(array)), axis)


def complex_product(left_pair, right_pair):
    highest = lax.Precision.HIGHEST
    real_part = jnp.dot(
        left_pair[0], right_pair[0], precision=highest, preferred_element_type=jnp.float32
    ) - jnp.dot(left_pair[1], right_pair[1], precision=highest, preferred_element_type=jnp.float32)
    imag_part = jnp.dot(
        left_pair[0], right_pair[1], precision=highest, preferred_element_type=jnp.float32
    ) + jnp.dot(left_pair[1], right_pair[0], precision=highest, preferred_element_type=jnp.float32)
    return jnp.stack([real_part, imag_part])


def structure(parent, node_count):
    node_index = jnp.arange(node_count, dtype=jnp.int32)
    reached = (parent[:, None] == node_index[None, :]).astype(jnp.int32)
    for level_index in range(node_count.bit_length()):
        reached = jnp.minimum(reached + jnp.dot(reached, reached), 1)
    diagonal_ones = (node_index[:, None] == node_index[None, :]).astype(jnp.int32)
    return jnp.minimum(diagonal_ones + reached + reached.T, 1)


def invert_pivot(pivot, sweeps):
    pivot_size = pivot.shape[-1]
    places = jnp.arange(pivot_size, dtype=jnp.int32)
    identity_real = (places[:, None] == places[None, :]).astype(jnp.float32)
    diag_real = jnp.diagonal(pivot[0])
    diag_imag = jnp.diagonal(pivot[1])
    modulus = diag_real * diag_real + diag_imag * diag_imag
    approx = jnp.stack(
        [
            identity_real * (diag_real / modulus)[None, :],
            identity_real * (-diag_imag / modulus)[None, :],
        ]
    )
    for sweep_index in range(sweeps):
        product = complex_product(pivot, approx)
        residue = jnp.stack([2.0 * identity_real - product[0], -product[1]])
        approx = complex_product(approx, residue)
    return approx


def body(hamiltonian, margin, pole_shift, row_map, parent):
    grid_rows = lax.axis_size("prow")
    grid_cols = lax.axis_size("pcol")
    my_row = lax.axis_index("prow")
    my_col = lax.axis_index("pcol")
    ham_block, over_block = (
        lax.all_to_all(hamiltonian, "pcol", split_axis=1, concat_axis=0, tiled=True),
        lax.all_to_all(margin, "pcol", split_axis=1, concat_axis=0, tiled=True),
    )
    block_height = ham_block.shape[0]
    block_width = ham_block.shape[1]
    local_rows = row_map - my_row * block_height
    ham_block = jnp.take(ham_block, local_rows, axis=0).astype(jnp.float32)
    over_block = jnp.take(over_block, local_rows, axis=0).astype(jnp.float32)
    matrix = jnp.stack([ham_block - pole_shift[0] * over_block, -pole_shift[1] * over_block])
    node_count = parent.shape[0]
    pattern = structure(parent, node_count)
    row_nodes = jnp.arange(block_height // SN, dtype=jnp.int32) * grid_rows + my_row
    col_nodes = jnp.arange(block_width // SN, dtype=jnp.int32) * grid_cols + my_col
    all_nodes = jnp.arange(node_count, dtype=jnp.int32)
    pick_rows = (row_nodes[:, None] == all_nodes[None, :]).astype(jnp.int32)
    pick_cols = (col_nodes[:, None] == all_nodes[None, :]).astype(jnp.int32)
    local_pattern = jnp.dot(jnp.dot(pick_rows, pattern), pick_cols.T)
    row_owner = jnp.repeat(row_nodes, SN)
    col_owner = jnp.repeat(col_nodes, SN)
    keep_mask = jnp.repeat(jnp.repeat(local_pattern, SN, axis=0), SN, axis=1).astype(jnp.float32)
    matrix = matrix * keep_mask[None]
    places = jnp.arange(SN, dtype=jnp.int32)
    identity_real = (places[:, None] == places[None, :]).astype(jnp.float32)
    identity_pair = jnp.stack([identity_real, jnp.zeros_like(identity_real)])
    for elimination in range(STEPS):
        owner_row = elimination % grid_rows
        owner_col = elimination % grid_cols
        row_slot = elimination // grid_rows * SN
        col_slot = elimination // grid_cols * SN
        is_owner = (my_row == owner_row) & (my_col == owner_col)
        pivot_here = jnp.where(
            is_owner, matrix[:, row_slot : row_slot + SN, col_slot : col_slot + SN], identity_pair
        )
        below_rows = row_owner > elimination
        below_mask = below_rows.astype(jnp.float32)[None, :, None]
        column_here = matrix[:, :, col_slot : col_slot + SN]
        inverse = broadcast(
            invert_pivot(pivot_here, NSI).astype(jnp.bfloat16), "prow", owner_row
        ).astype(jnp.float32)
        factor = broadcast(
            (complex_product(column_here, inverse) * below_mask).astype(jnp.bfloat16),
            "pcol",
            owner_col,
        ).astype(jnp.float32)
        beyond = (col_owner > elimination).astype(jnp.float32)[None, None, :]
        row_panel = broadcast(
            matrix[:, row_slot : row_slot + SN, :].astype(jnp.bfloat16), "prow", owner_row
        ).astype(jnp.float32)
        matrix = matrix - complex_product(factor, row_panel * beyond)
        current = matrix[:, :, col_slot : col_slot + SN]
        written = jnp.where(below_rows[None, :, None] & (my_col == owner_col), factor, current)
        matrix = matrix.at[:, :, col_slot : col_slot + SN].set(written)
    return matrix


def solution(mesh):
    return jax.shard_map(
        body,
        mesh=mesh,
        in_specs=(P(("prow", "pcol"), None), P(("prow", "pcol"), None), P("pole"), P("prow"), P()),
        out_specs=P("pole", "prow", "pcol"),
        check_vma=False,
    )
```

profile of v0, /device:TPU:0, one launch (start us, length us, event | category | flops | bytes accessed | tf_op | source)
XLA Modules:
  0.0 565.9 jit_solution(4958714103424705375)
XLA Ops:
  6.5 3.3 copy.30
  9.8 6.3 %all-to-all-start = ((bf16[192,4,1536]{2,0,1:T(8,128)(2,1)}), bf16[192,4,1536]{2,0,1:T(8,128)(2,1)S(1)}, u32[]{:S(2)}, u32[]{:S(2)}) async-start(bf16[192,4,1536]{2,0,1:T(8,128)(2,1)} %bitcast.422), calls=%async_computation | async-start | bytes 4718592 | tf_op jit(solution)/shard_map/all_to_all | solution.py:62
  17.5 3.3 copy.29
  20.8 49.2 %all-to-all-done = bf16[192,4,1536]{2,0,1:T(8,128)(2,1)S(1)} async-done(((bf16[192,4,1536]{2,0,1:T(8,128)(2,1)}), bf16[192,4,1536]{2,0,1:T(8,128)(2,1)S(1)}, u32[]{:S(2)}, u32[]{:S(2)}) %all-to-all-start) | async-done | bytes 2359328 | tf_op jit(solution)/shard_map/all_to_all | solution.py:62
  70.0 4.5 all-to-all-start.1
  75.9 2.5 broadcast_in_dim.100
  78.4 6.1 %copy.23 = f32[768,1536]{1,0:T(8,128)} copy(f32[768,1536]{0,1:T(8,128)} %bitcast.420) | data formatting | bytes 9437184 | tf_op jit(solution)/shard_map/convert_element_type | solution.py:81
  86.2 3.8 gather_fusion.6
  90.0 37.9 %all-to-all-done.1 = bf16[192,4,1536]{2,0,1:T(8,128)(2,1)} async-done(((bf16[192,4,1536]{2,0,1:T(8,128)(2,1)}), bf16[192,4,1536]{2,0,1:T(8,128)(2,1)}, u32[]{:S(2)}, u32[]{:S(2)}) %all-to-all-start.1) | async-done | bytes 2359328 | tf_op jit(solution)/shard_map/all_to_all | solution.py:63
  127.9 7.9 %gather_fusion.7 = bf16[768,1536]{1,0:T(8,128)(2,1)} fusion(bf16[768,1536]{1,0:T(8,128)(2,1)} %bitcast.4, s32[1024]{0:T(1024)S(1)} %pad_clamp_fusion), kind=kCustom, calls=%fused_computation.1.clone | custom fusion | bytes 4721664 | tf_op jit(solution)/shard_map/jit(_take)/gather | solution.py:69
  135.8 8.5 %fusion.1 = (f32[1,768,1536]{2,1,0:T(8,128)}, f32[1,768,1536]{2,1,0:T(8,128)}) fusion(bf16[768,1536]{1,0:T(8,128)(2,1)} %gather_fusion.6, f32[]{:T(128)} %bitcast.2, pred[768]{0:T(1024)(128)(4,1)S(1)} %get-tuple-element.52, bf16[768,1536]{1,0:T(8,128)(2,1)} %gather_fusion.7, f32[]{:T(128)} %bitcast.6), kind=kLoop, calls=%fused_computation.15 | loop fusion | flops 8257536 | bytes 14156552 | tf_op jit(solution)/shard_map/stack | solution.py:70
  144.3 8.8 %maximum_multiply_fusion = f32[2,768,1536]{2,1,0:T(8,128)} fusion(f32[1,768,1536]{2,1,0:T(8,128)} %get-tuple-element.55, f32[1,768,1536]{2,1,0:T(8,128)} %get-tuple-element.54, f32[768,1536]{1,0:T(8,128)S(1)} %copy-done), kind=kLoop, calls=%fused_computation.8 | loop fusion | flops 4718592 | bytes 23592960 | tf_op jit(solution)/shard_map/mul | solution.py:82
  153.1 2.4 fusion.47
  155.5 0.9 convert_select_fusion.2
  156.4 1.2 gather_fusion
  157.6 1.2 gather_fusion.1
  165.7 0.6 maximum_select_fusion
  166.8 54.8 %all-reduce.21.cloned.1.call-done = (bf16[2,128,1536]{2,1,0:T(8,128)(2,1)}, bf16[2,128,128]{2,1,0:T(8,128)(2,1)}) async-done(((bf16[2,128,1536]{2,1,0:T(8,128)(2,1)}, bf16[2,128,128]{2,1,0:T(8,128)(2,1)}), (bf16[2,128,1536]{2,1,0:T(8,128)(2,1)}, bf16[2,128,128]{2,1,0:T(8,128)(2,1)})) %all-reduce.21.cloned.1.call-update) | async-done | bytes 851984 | tf_op jit(solution)/shard_map/psum | solution.py:13
  221.6 1.4 fusion.64
  222.9 1.3 fusion.63
  224.3 1.3 fusion.8
  225.6 1.3 fusion.7
  226.9 0.9 fusion.62
  228.1 36.2 %all-reduce.11.cloned.1.call-done = bf16[2,768,128]{2,1,0:T(8,128)(2,1)} async-done(((bf16[2,768,128]{2,1,0:T(8,128)(2,1)}), bf16[2,768,128]{2,1,0:T(8,128)(2,1)}) %all-reduce.11.cloned.1.call-update) | async-done | bytes 393232 | tf_op jit(solution)/shard_map/psum | solution.py:13
  264.3 3.1 fusion.54
  267.4 2.1 fusion.55
  269.5 2.1 subtract_bitcast_fusion.2
  271.6 2.1 add_bitcast_fusion.2
  274.6 5.4 maximum_subtract_fusion
  280.0 2.2 constant_dynamic-update-slice_fusion.1
  282.2 1.2 gather_fusion.2
  283.5 1.2 gather_fusion.3
  291.5 2.4 fusion.48
  293.9 0.6 maximum_select_fusion.1
  294.8 55.5 %all-reduce.19.cloned.1.call-done = (bf16[2,128,1536]{2,1,0:T(8,128)(2,1)}, bf16[2,128,128]{2,1,0:T(8,128)(2,1)}) async-done(((bf16[2,128,1536]{2,1,0:T(8,128)(2,1)}, bf16[2,128,128]{2,1,0:T(8,128)(2,1)}), (bf16[2,128,1536]{2,1,0:T(8,128)(2,1)}, bf16[2,128,128]{2,1,0:T(8,128)(2,1)})) %all-reduce.19.cloned.1.call-update) | async-done | bytes 851984 | tf_op jit(solution)/shard_map/psum | solution.py:13
  350.2 1.1 fusion.66
  351.4 1.1 fusion.65
  352.5 1.1 fusion.6
  353.5 1.1 fusion.5
  354.6 0.9 fusion.61
  356.0 36.0 %all-reduce.13.cloned.1.call-done = bf16[2,768,128]{2,1,0:T(8,128)(2,1)} async-done(((bf16[2,768,128]{2,1,0:T(8,128)(2,1)}), bf16[2,768,128]{2,1,0:T(8,128)(2,1)}) %all-reduce.13.cloned.1.call-update) | async-done | bytes 393232 | tf_op jit(solution)/shard_map/psum | solution.py:13
  392.0 3.1 fusion.56
  395.1 2.1 fusion.57
  397.1 4.4 subtract_bitcast_fusion.1
  401.5 4.3 add_bitcast_fusion.1
  405.8 12.4 %maximum_subtract_fusion.1 = f32[2,768,1536]{2,1,0:T(8,128)} fusion(f32[2,768,1536]{2,1,0:T(8,128)} %get-tuple-element.50, f32[1,768,1536]{2,1,0:T(8,128)} %add_bitcast_fusion.1, f32[1,768,1536]{2,1,0:T(8,128)} %subtract_bitcast_fusion.1), kind=kLoop, calls=%fused_computation.10 | loop fusion | flops 4718592 | bytes 28311552 | tf_op jit(solution)/shard_map/sub | solution.py:110
  418.2 2.2 constant_dynamic-update-slice_fusion
  420.5 1.2 gather_fusion.4
  421.7 1.2 gather_fusion.5
  429.8 2.4 fusion.49
  432.1 0.6 maximum_select_fusion.2
  433.2 55.3 %all-reduce.17.cloned.1.call-done = (bf16[2,128,1536]{2,1,0:T(8,128)(2,1)}, bf16[2,128,128]{2,1,0:T(8,128)(2,1)}) async-done(((bf16[2,128,1536]{2,1,0:T(8,128)(2,1)}, bf16[2,128,128]{2,1,0:T(8,128)(2,1)}), (bf16[2,128,1536]{2,1,0:T(8,128)(2,1)}, bf16[2,128,128]{2,1,0:T(8,128)(2,1)})) %all-reduce.17.cloned.1.call-update) | async-done | bytes 851984 | tf_op jit(solution)/shard_map/psum | solution.py:13
  488.5 1.1 fusion.68
  489.7 1.1 fusion.67
  490.7 1.1 fusion.4
  491.8 1.1 fusion.3
  492.9 0.9 fusion.60
  494.0 36.3 %all-reduce.15.cloned.1.call-done = bf16[2,768,128]{2,1,0:T(8,128)(2,1)} async-done(((bf16[2,768,128]{2,1,0:T(8,128)(2,1)}), bf16[2,768,128]{2,1,0:T(8,128)(2,1)}) %all-reduce.15.cloned.1.call-update) | async-done | bytes 393232 | tf_op jit(solution)/shard_map/psum | solution.py:13
  530.3 3.1 fusion.58
  533.4 2.1 fusion.59
  535.4 4.4 subtract_bitcast_fusion
  539.8 4.3 add_bitcast_fusion
  544.1 12.4 %maximum_subtract_fusion.2 = f32[2,768,1536]{2,1,0:T(8,128)} fusion(f32[2,768,1536]{2,1,0:T(8,128)} %get-tuple-element.48, f32[1,768,1536]{2,1,0:T(8,128)} %add_bitcast_fusion, f32[1,768,1536]{2,1,0:T(8,128)} %subtract_bitcast_fusion), kind=kLoop, calls=%fused_computation.11 | loop fusion | flops 4718592 | bytes 28311552 | tf_op jit(solution)/shard_map/sub | solution.py:110
  556.5 2.2 fusion.50
  (198 shorter events, 26.0 us)
Async XLA Ops:
  6.5 9.6 %copy-start.7 = (s32[48]{0:T(128)S(1)}, s32[48]{0:T(128)}, u32[]{:S(2)}) copy-start(s32[48]{0:T(128)} %param.17) | copy-start | bytes 580
  9.8 60.1 %all-to-all-start = ((bf16[192,4,1536]{2,0,1:T(8,128)(2,1)}), bf16[192,4,1536]{2,0,1:T(8,128)(2,1)S(1)}, u32[]{:S(2)}, u32[]{:S(2)}) async-start(bf16[192,4,1536]{2,0,1:T(8,128)(2,1)} %bitcast.422), calls=%async_computation | async-start | bytes 4718592 | tf_op jit(solution)/shard_map/all_to_all | solution.py:62
  70.0 57.9 %all-to-all-start.1 = ((bf16[192,4,1536]{2,0,1:T(8,128)(2,1)}), bf16[192,4,1536]{2,0,1:T(8,128)(2,1)}, u32[]{:S(2)}, u32[]{:S(2)}) async-start(bf16[192,4,1536]{2,0,1:T(8,128)(2,1)} %bitcast.421), calls=%async_computation.1 | async-start | bytes 4718592 | tf_op jit(solution)/shard_map/all_to_all | solution.py:63
  74.5 147.0 %all-reduce.21.cloned.1.call-start = ((), (), s32[]{:S(2)}) async-start(), calls=%async_computation.7 | async-start | bytes 1703936 | tf_op jit(solution)/shard_map/psum | solution.py:13
  78.4 6.1 %copy-start.9 = (f32[2]{0:T(128)S(1)}, f32[2]{0:T(128)}, u32[]{:S(2)}) copy-start(f32[2]{0:T(128)} %param.15) | copy-start | bytes 28
  78.4 7.5 %copy-start.8 = (s32[768]{0:T(1024)S(1)}, s32[768]{0:T(1024)}, u32[]{:S(2)}) copy-start(s32[768]{0:T(1024)} %param.16) | copy-start | bytes 9220
  135.8 8.5 %copy-start = (f32[768,1536]{1,0:T(8,128)S(1)}, f32[768,1536]{1,0:T(8,128)}, u32[]{:S(2)}) copy-start(f32[768,1536]{1,0:T(8,128)} %copy.23) | copy-start | bytes 14155780
  166.4 97.9 %all-reduce.11.cloned.1.call-start = ((), (), s32[]{:S(2)}) async-start(), calls=%async_computation.2 | async-start | bytes 786432 | tf_op jit(solution)/shard_map/psum | solution.py:13
  221.6 6.3 %copy-start.4 = (bf16[2,128,1536]{2,1,0:T(8,128)(2,1)S(1)}, bf16[2,128,1536]{2,1,0:T(8,128)(2,1)}, u32[]{:S(2)}) copy-start(bf16[2,128,1536]{2,1,0:T(8,128)(2,1)} %get-tuple-element.46) | copy-start | bytes 2359300
  227.8 122.4 %all-reduce.19.cloned.1.call-start = ((), (), s32[]{:S(2)}) async-start(), calls=%async_computation.6 | async-start | bytes 1703936 | tf_op jit(solution)/shard_map/psum | solution.py:13
  264.3 3.1 copy-start.1
  269.4 4.3 slice-start
  269.4 4.3 slice-start.2
  269.4 4.6 slice-start.4
  271.6 2.7 slice-start.1
  271.6 2.9 slice-start.3
  271.6 3.0 slice-start.5
  294.6 97.4 %all-reduce.13.cloned.1.call-start = ((), (), s32[]{:S(2)}) async-start(), calls=%async_computation.3 | async-start | bytes 786432 | tf_op jit(solution)/shard_map/psum | solution.py:13
  350.2 5.6 copy-start.5
  355.6 132.9 %all-reduce.17.cloned.1.call-start = ((), (), s32[]{:S(2)}) async-start(), calls=%async_computation.5 | async-start | bytes 1703936 | tf_op jit(solution)/shard_map/psum | solution.py:13
  392.0 3.1 copy-start.2
  432.8 97.5 %all-reduce.15.cloned.1.call-start = ((), (), s32[]{:S(2)}) async-start(), calls=%async_computation.4 | async-start | bytes 786432 | tf_op jit(solution)/shard_map/psum | solution.py:13
  488.5 5.3 copy-start.6
  530.3 3.1 copy-start.3
Sparse Core Ops, SparseCore 0:
  166.5 55.0 all-reduce.20
  228.0 36.2 all-reduce.10
  294.7 55.4 all-reduce.18
  355.7 36.2 all-reduce.12
  432.9 55.5 all-reduce.16
  494.0 36.2 all-reduce.14
where the time goes:
time: 576 us; the launch traced here: 566 us
  waiting for transfers between devices  361 us (63%)
  matrix products  72.4 us (13%)
  other arithmetic  67.5 us (12%)
  local copies, waits for them, and re-layouts  37.2 us (6%)
  between operations  15.9 us (3%)
  starting transfers between devices  11.7 us (2%)
    psum x6, waiting for transfers between devices, broadcast(): return lax.psum(jnp.where(mine, array, jnp.zeros_like(array)), axis)  274 us
    all_to_all x1, waiting for transfers between devices, body(): lax.all_to_all(hamiltonian, 'pcol', split_axis=1, concat_axis=0, tiled=True)  49.2 us
    all_to_all x1, waiting for transfers between devices, body(): lax.all_to_all(margin, 'pcol', split_axis=1, concat_axis=0, tiled=True)  37.9 us
    sub x3, other arithmetic, body(): matrix = matrix - complex_product(factor, row_panel * beyond)  30.2 us
    dot_general x30, matrix products, complex_product(): jnp.dot(left_pair[1], right_pair[1], precision=highest, preferred_element...  19.2 us
    dot_general x30, matrix products, complex_product(): jnp.dot(left_pair[1], right_pair[0], precision=highest, preferred_element...  19.2 us
    dot_general x30, matrix products, complex_product(): jnp.dot(left_pair[0], right_pair[0], precision=highest, preferred_element...  17.7 us
    dot_general x30, matrix products, complex_product(): jnp.dot(left_pair[0], right_pair[1], precision=highest, preferred_element...  14.5 us
  transfers between devices with their start and end apart: 8, of which 8 were waited for; matrix products, arithmetic and copies ran while one was open for 4% of the time, Pallas kernels for 0%

commit v1 on v0

v1 whole, which is shorter than its diff:
```python
import functools

import jax
import jax.numpy as jnp
from jax import lax
from jax.experimental import pallas as pl
from jax.experimental.pallas import tpu as pltpu
from jax.sharding import PartitionSpec as P

SN = 128
STEPS = 3
NSI = 4
PAN = STEPS * SN
VMEM_LIMIT = 50 * 1024 * 1024
MESH = pl.DeviceIdType.MESH


def structure(parent, node_count):
    node_index = jnp.arange(node_count, dtype=jnp.int32)
    reached = (parent[:, None] == node_index[None, :]).astype(jnp.bfloat16)
    for level_index in range(node_count.bit_length()):
        hop = jnp.dot(reached, reached, preferred_element_type=jnp.float32)
        reached = jnp.minimum(reached.astype(jnp.float32) + hop, 1.0).astype(jnp.bfloat16)
    reached = reached.astype(jnp.float32)
    same = (node_index[:, None] == node_index[None, :]).astype(jnp.float32)
    return jnp.minimum(same + reached + reached.T, 1.0)


def line_gather_kernel(n, mine_ref, out_ref, local_sem, up_sem, down_sem, recv_sem):
    me = lax.axis_index("pcol")
    row = lax.axis_index("prow")
    pole = lax.axis_index("pole")
    barrier = pltpu.get_barrier_semaphore()

    @pl.when(me + 1 < n)
    def _():
        pl.semaphore_signal(barrier, inc=1, device_id=(pole, row, me + 1), device_id_type=MESH)

    @pl.when(me >= 1)
    def _():
        pl.semaphore_signal(barrier, inc=1, device_id=(pole, row, me - 1), device_id_type=MESH)

    pl.semaphore_wait(barrier, jnp.where(me + 1 < n, 1, 0) + jnp.where(me >= 1, 1, 0))

    local = pltpu.make_async_copy(mine_ref, out_ref.at[me], local_sem)
    local.start()
    local.wait()

    def send(slot, target, sems):
        return pltpu.make_async_remote_copy(
            src_ref=out_ref.at[slot],
            dst_ref=out_ref.at[slot],
            send_sem=sems.at[slot],
            recv_sem=recv_sem.at[slot],
            device_id=(pole, row, target),
            device_id_type=MESH,
        )

    for step in range(n):
        low = me - step
        high = me + step
        if step:

            @pl.when(low >= 0)
            def _():
                send(low, me, up_sem).wait_recv()

        @pl.when((low >= 0) & (me + 1 < n))
        def _():
            send(low, me + 1, up_sem).start()

        if step:

            @pl.when(high < n)
            def _():
                send(high, me, down_sem).wait_recv()

        @pl.when((high < n) & (me >= 1))
        def _():
            send(high, me - 1, down_sem).start()

    for step in range(n):
        low = me - step
        high = me + step

        @pl.when((low >= 0) & (me + 1 < n))
        def _():
            send(low, me + 1, up_sem).wait_send()

        @pl.when((high < n) & (me >= 1))
        def _():
            send(high, me - 1, down_sem).wait_send()


def line_gather(mine, n):
    return pl.pallas_call(
        functools.partial(line_gather_kernel, n),
        out_shape=jax.ShapeDtypeStruct((n,) + mine.shape, mine.dtype),
        in_specs=[pl.BlockSpec(memory_space=pl.ANY)],
        out_specs=pl.BlockSpec(memory_space=pl.ANY),
        scratch_shapes=[
            pltpu.SemaphoreType.DMA,
            pltpu.SemaphoreType.DMA((n,)),
            pltpu.SemaphoreType.DMA((n,)),
            pltpu.SemaphoreType.DMA((n,)),
        ],
        compiler_params=pltpu.CompilerParams(collective_id=0, has_side_effects=True),
        cost_estimate=pl.CostEstimate(flops=0, bytes_accessed=40_000_000, transcendentals=0),
    )(mine)


def tree_kernel(n, groups, pcols, panel_ref, *rest):
    items = groups + STEPS
    outs = rest[:items]
    local_sem, send_sem, recv_sem = rest[items:]
    me = lax.axis_index("prow")
    col = lax.axis_index("pcol")
    pole = lax.axis_index("pole")
    bits = n.bit_length() - 1
    bit = lambda value, b: (value // (1 << b)) % 2
    partner = lambda b: me + (1 << b) * (1 - 2 * bit(me, b))
    barrier = pltpu.get_barrier_semaphore()
    for b in range(bits):
        pl.semaphore_signal(barrier, inc=1, device_id=(pole, partner(b), col), device_id_type=MESH)
    pl.semaphore_wait(barrier, bits)
    roots = [(col + j * pcols) % n for j in range(groups)] + list(range(STEPS))
    forward = list(range(1, bits)) + [0]
    backward = list(range(bits - 1, 0, -1)) + [0]
    orders = [backward if i % 2 else forward for i in range(items)]
    for i in range(items):

        @pl.when(me == roots[i])
        def _():
            source = panel_ref if i < groups else panel_ref.at[:, 0:SN]
            copy = pltpu.make_async_copy(source, outs[i], local_sem.at[i])
            copy.start()
            copy.wait()

    def send(i, stage):
        return pltpu.make_async_remote_copy(
            src_ref=outs[i],
            dst_ref=outs[i],
            send_sem=send_sem.at[i, stage],
            recv_sem=recv_sem.at[i],
            device_id=(pole, partner(orders[i][stage]), col),
            device_id_type=MESH,
        )

    def relative(i, stage):
        return (bit(me, orders[i][stage]) + bit(roots[i], orders[i][stage])) % 2

    def later(i, stage):
        total = 0
        for k in range(stage, bits):
            total = total + relative(i, k)
        return total

    sequence = list(range(groups, items)) + list(range(groups))
    for stage in range(bits):
        for i in sequence:

            @pl.when(later(i, stage) == 0)
            def _():
                send(i, stage).start()

        for i in sequence:

            @pl.when((relative(i, stage) == 1) & (later(i, stage) == 1))
            def _():
                send(i, stage).wait_recv()

    for stage in range(bits):
        for i in sequence:

            @pl.when(later(i, stage) == 0)
            def _():
                send(i, stage).wait_send()


def tree(panel, n, groups, pcols):
    bits = n.bit_length() - 1
    items = groups + STEPS
    shapes = [jax.ShapeDtypeStruct(panel.shape, panel.dtype)] * groups + [
        jax.ShapeDtypeStruct((2, SN, PAN), panel.dtype)
    ] * STEPS
    return pl.pallas_call(
        functools.partial(tree_kernel, n, groups, pcols),
        out_shape=shapes,
        in_specs=[pl.BlockSpec(memory_space=pl.ANY)],
        out_specs=[pl.BlockSpec(memory_space=pl.ANY)] * items,
        scratch_shapes=[
            pltpu.SemaphoreType.DMA((items,)),
            pltpu.SemaphoreType.DMA((items, bits)),
            pltpu.SemaphoreType.DMA((items,)),
        ],
        compiler_params=pltpu.CompilerParams(collective_id=1, has_side_effects=True),
        cost_estimate=pl.CostEstimate(flops=0, bytes_accessed=60_000_000, transcendentals=0),
    )(panel)


def real_form(pair):
    left, right = pair[:, :SN], pair[:, SN:]
    return jnp.concatenate([pair, jnp.concatenate([-right, left], axis=1)], axis=0)


def panel_kernel(chunk, high, wide, pivot_ref, node_ref, rows_ref, factor_ref, real_ref, imag_ref, inv, step_b, piv):
    exact = functools.partial(
        jnp.dot, precision=lax.Precision.HIGHEST, preferred_element_type=jnp.float32
    )
    piv[...] = pivot_ref[...]
    place_r = lax.broadcasted_iota(jnp.int32, (SN, SN), 0)
    place_c = lax.broadcasted_iota(jnp.int32, (SN, SN), 1)
    eye = (place_r == place_c).astype(jnp.float32)
    zero = jnp.zeros_like(eye)
    two = 2.0 * real_form(jnp.concatenate([eye, zero], axis=1))
    pairs = [(0, 1), (0, 2), (1, 2)]
    for t in range(STEPS):
        here = slice(t * SN, (t + 1) * SN)
        cols = slice(2 * t * SN, 2 * (t + 1) * SN)
        pivot = piv[here, cols]
        full = real_form(pivot)
        diag_r = jnp.sum(eye * pivot[:, :SN], axis=0, keepdims=True)
        diag_i = jnp.sum(eye * pivot[:, SN:], axis=0, keepdims=True)
        modulus = diag_r * diag_r + diag_i * diag_i
        approx = real_form(
            jnp.concatenate([eye * (diag_r / modulus), eye * (-diag_i / modulus)], axis=1)
        )
        for sweep in range(NSI):
            approx = exact(approx, two - exact(full, approx))
        inv[t] = approx.astype(jnp.bfloat16)
        if t + 1 < STEPS:
            below = slice((t + 1) * SN, STEPS * SN)
            factor = exact(piv[below, cols], approx)
            for t2 in range(t + 1, STEPS):
                cols2 = slice(2 * t2 * SN, 2 * (t2 + 1) * SN)
                link = real_form(piv[here, cols2])
                step_b[pairs.index((t, t2))] = link.astype(jnp.bfloat16)
                piv[below, cols2] = piv[below, cols2] - exact(factor, link)

    def work(start):
        span = pl.ds(start, chunk)
        node = node_ref[span, :]
        blocks = [rows_ref[span, 2 * t * SN : 2 * (t + 1) * SN] for t in range(STEPS)]
        factors = []
        kept = []
        for t in range(STEPS):
            below = node > t
            now = blocks[t].astype(jnp.bfloat16)
            factor = jnp.dot(now, inv[t], preferred_element_type=jnp.float32)
            factor = jnp.where(below, factor, 0.0).astype(jnp.bfloat16)
            for t2 in range(t + 1, STEPS):
                blocks[t2] = blocks[t2] - jnp.dot(
                    factor, step_b[pairs.index((t, t2))], preferred_element_type=jnp.float32
                )
            factors.append(factor)
            kept.append(jnp.where(below, blocks[t], 0.0))
        return factors, kept

    @pl.loop(0, high // chunk)
    def _(k):
        start = pl.multiple_of(k * chunk, chunk)
        factors, kept = work(start)
        for t in range(STEPS):
            factor_ref[pl.ds(start, chunk), 2 * t * SN : 2 * (t + 1) * SN] = factors[t]

    @pl.loop(0, wide // chunk)
    def _(k):
        start = pl.multiple_of(k * chunk, chunk)
        factors, kept = work(pl.multiple_of(high + start, chunk))
        for t in range(STEPS):
            re, im = kept[t][:, :SN], kept[t][:, SN:]
            span = pl.ds(start, chunk)
            cols = slice(2 * t * SN, 2 * (t + 1) * SN)
            real_ref[span, cols] = jnp.concatenate([re, -im], axis=1).astype(jnp.bfloat16)
            imag_ref[span, cols] = jnp.concatenate([im, re], axis=1).astype(jnp.bfloat16)


def panels(pivot, nodes, rows, high, wide):
    chunk = 256
    bf = jnp.bfloat16
    return pl.pallas_call(
        functools.partial(panel_kernel, chunk, high, wide),
        out_shape=[
            jax.ShapeDtypeStruct((high, 2 * PAN), bf),
            jax.ShapeDtypeStruct((wide, 2 * PAN), bf),
            jax.ShapeDtypeStruct((wide, 2 * PAN), bf),
        ],
        in_specs=[pl.BlockSpec(memory_space=pltpu.VMEM)] * 3,
        out_specs=[pl.BlockSpec(memory_space=pltpu.VMEM)] * 3,
        scratch_shapes=[
            pltpu.VMEM((STEPS, 2 * SN, 2 * SN), bf),
            pltpu.VMEM((3, 2 * SN, 2 * SN), bf),
            pltpu.VMEM((PAN, 2 * PAN), jnp.float32),
        ],
        compiler_params=pltpu.CompilerParams(vmem_limit_bytes=VMEM_LIMIT),
        cost_estimate=pl.CostEstimate(
            flops=20_000_000_000, bytes_accessed=20_000_000, transcendentals=0
        ),
    )(pivot, nodes, rows)


def update_kernel(tile, shift_ref, keep_ref, block_ref, map_ref, node_ref, factor_ref, real_ref, imag_ref, own_ref, mine_ref, out_ref, pick):
    j = pl.program_id(0)
    high = map_ref.shape[0]
    blocks, _, share, _ = block_ref.shape

    @pl.when(j == 0)
    def _():
        place = lax.broadcasted_iota(jnp.int32, (high, high), 1)
        pick[...] = (place == map_ref[...]).astype(jnp.bfloat16)

    nt = (((1,), (1,)), ((), ()))
    factor = factor_ref[...]
    ham = jnp.dot(
        pick[...], block_ref[:, 0].reshape(high, tile), preferred_element_type=jnp.float32
    )
    over = jnp.dot(
        pick[...], block_ref[:, 1].reshape(high, tile), preferred_element_type=jnp.float32
    )
    up_r = lax.dot_general(factor, real_ref[...], nt, preferred_element_type=jnp.float32)
    up_i = lax.dot_general(factor, imag_ref[...], nt, preferred_element_type=jnp.float32)
    zr, zi = shift_ref[0], shift_ref[1]
    for a in range(high // SN):
        for b in range(tile // SN):
            ra, cb = slice(a * SN, (a + 1) * SN), slice(b * SN, (b + 1) * SN)
            keep = keep_ref[a, j * (tile // SN) + b] > 0.5
            h, s = ham[ra, cb], over[ra, cb]
            out_ref[0, ra, cb] = jnp.where(keep, h - zr * s, 0.0) - up_r[ra, cb]
            out_ref[1, ra, cb] = jnp.where(keep, -zi * s, 0.0) - up_i[ra, cb]

    @pl.when(j == 0)
    def _():
        take = node_ref[...] > mine_ref[0]
        for p in range(2):
            own = own_ref[:, p * SN : (p + 1) * SN].astype(jnp.float32)
            out_ref[p, :, 0:SN] = jnp.where(take, own, out_ref[p, :, 0:SN])


def update(shift, keep, block, row_places, row_owner, factor, real, imag, own, mine):
    blocks, _, share, wide = block.shape
    high = blocks * share
    tile = 256
    smem = pl.BlockSpec(memory_space=pltpu.SMEM)
    whole = lambda shape: pl.BlockSpec(shape, lambda j: (0,) * len(shape))
    return pl.pallas_call(
        functools.partial(update_kernel, tile),
        grid=(wide // tile,),
        out_shape=jax.ShapeDtypeStruct((2, high, wide), jnp.float32),
        in_specs=[
            smem,
            smem,
            pl.BlockSpec((blocks, 2, share, tile), lambda j: (0, 0, 0, j)),
            whole((high, 1)),
            whole((high, 1)),
            whole((high, 2 * PAN)),
            pl.BlockSpec((tile, 2 * PAN), lambda j: (j, 0)),
            pl.BlockSpec((tile, 2 * PAN), lambda j: (j, 0)),
            whole((high, 2 * SN)),
            smem,
        ],
        out_specs=pl.BlockSpec((2, high, tile), lambda j: (0, 0, j)),
        scratch_shapes=[pltpu.VMEM((high, high), jnp.bfloat16)],
        compiler_params=pltpu.CompilerParams(vmem_limit_bytes=VMEM_LIMIT),
        cost_estimate=pl.CostEstimate(
            flops=8 * high * wide * PAN, bytes_accessed=20_000_000, transcendentals=0
        ),
    )(shift, keep, block, row_places, row_owner, factor, real, imag, own, mine)


def body(hamiltonian, margin, pole_shift, row_map, parent):
    grid_rows = lax.axis_size("prow")
    grid_cols = lax.axis_size("pcol")
    my_row = lax.axis_index("prow")
    my_col = lax.axis_index("pcol")
    share, total = hamiltonian.shape
    wide = total // grid_cols
    high = row_map.shape[0]
    node_count = parent.shape[0]

    both = jnp.stack(
        [
            jnp.stack([m[:, c * wide : (c + 1) * wide] for m in (hamiltonian, margin)])
            for c in range(grid_cols)
        ]
    )
    block = lax.all_to_all(both, "pcol", split_axis=0, concat_axis=0, tiled=True)

    edge = jnp.stack(
        [
            jnp.concatenate([m[:, t * wide : t * wide + SN] for t in range(STEPS)], axis=1)
            for m in (hamiltonian, margin)
        ]
    )
    gathered = line_gather(edge, grid_cols)
    gathered = gathered.transpose(1, 0, 2, 3).reshape(2, high, PAN)
    row_places = row_map - my_row * high
    pick = (row_places[:, None] == jnp.arange(high, dtype=jnp.int32)[None, :]).astype(jnp.bfloat16)
    panel = jnp.einsum("nm,pmk->pnk", pick, gathered, preferred_element_type=jnp.float32).astype(
        jnp.bfloat16
    )
    groups = next(g for g in range(1, grid_rows + 1) if g * grid_cols % grid_rows == 0)
    spread = tree(panel, grid_rows, groups, grid_cols)

    slots = []
    for k in range(wide // SN):
        item = spread[k % groups]
        if grid_rows % grid_cols == 0:
            slot = k * grid_cols // grid_rows
            slots.append(item[:, slot * SN : (slot + 1) * SN])
        else:
            slot = (k * grid_cols + my_col) // grid_rows
            slots.append(lax.dynamic_slice_in_dim(item, slot * SN, SN, axis=1))
    pattern = structure(parent, node_count)
    row_nodes = jnp.arange(high // SN, dtype=jnp.int32) * grid_rows + my_row
    col_nodes = jnp.arange(wide // SN, dtype=jnp.int32) * grid_cols + my_col
    all_nodes = jnp.arange(node_count, dtype=jnp.int32)
    pick_rows = (row_nodes[:, None] == all_nodes[None, :]).astype(jnp.float32)
    pick_cols = (col_nodes[:, None] == all_nodes[None, :]).astype(jnp.float32)
    keep = jnp.dot(jnp.dot(pick_rows, pattern), pick_cols.T)

    def shifted(raw, owners):
        rows = raw.shape[1]
        mask = jnp.dot(
            (owners[:, None] == all_nodes[None, :]).astype(jnp.float32), pattern[:, :STEPS]
        )
        mask = jnp.repeat(mask, SN, axis=0)[:, :, None]
        ham = raw[0].astype(jnp.float32).reshape(rows, STEPS, SN)
        over = raw[1].astype(jnp.float32).reshape(rows, STEPS, SN)
        real = jnp.where(mask > 0.5, ham - pole_shift[0] * over, 0.0)
        imag = jnp.where(mask > 0.5, -pole_shift[1] * over, 0.0)
        return jnp.stack([real, imag], axis=2).reshape(rows, 2 * PAN)

    pivot = shifted(jnp.concatenate(spread[groups:], axis=1), all_nodes[:STEPS])
    owners = jnp.concatenate([row_nodes, col_nodes])
    rows = shifted(jnp.concatenate([panel] + slots, axis=1), owners)
    nodes = jnp.repeat(owners, SN)[:, None]
    factor, real, imag = panels(pivot, nodes, rows, high, wide)
    step = jnp.minimum(my_col, STEPS - 1)
    own = lax.dynamic_slice_in_dim(factor, step * 2 * SN, 2 * SN, axis=1)
    mine = jnp.where(my_col < STEPS, my_col, node_count).astype(jnp.int32).reshape(1)
    return update(
        pole_shift, keep, block, row_places[:, None], nodes[:high], factor, real, imag, own, mine
    )


def solution(mesh):
    return jax.shard_map(
        body,
        mesh=mesh,
        in_specs=(P(("prow", "pcol"), None), P(("prow", "pcol"), None), P("pole"), P("prow"), P()),
        out_specs=P("pole", "prow", "pcol"),
        check_vma=False,
    )
```

time: 576 us -> 342 us (0.59)
  the two profiles are of different devices: /device:TPU:0 before, /device:TPU:7 now
where the time goes in v1:
time: 342 us; the launch traced here: 341 us
  Pallas kernels  249 us (73%)
  local copies, waits for them, and re-layouts  64.2 us (19%)
  other arithmetic  17.9 us (5%)
  starting transfers between devices  5 us (1%)
  matrix products  4.31 us (1%)
    pallas_call x1, Pallas kernels, line_gather(): pl.pallas_call(functools.partial(line_gather_kernel, n), out_shape=jax.Sh...  121 us
    pallas_call x1, Pallas kernels, tree(): pl.pallas_call(functools.partial(tree_kernel, n, groups, pcols), out_shap...  89.7 us
    pallas_call x1, Pallas kernels, panels(): pl.pallas_call(functools.partial(panel_kernel, chunk, high, wide), out_sh...  25.4 us
    unnamed x39, local copies, waits for them, and re-layouts  21.6 us
    another operation x2, local copies, waits for them, and re-layouts, shifted(): return jnp.stack([real, imag], axis=2).reshape(rows, 2 * PAN)  13.3 us
    pallas_call x1, Pallas kernels, update(): pl.pallas_call(functools.partial(update_kernel, tile), grid=(wide // tile...  12.7 us
    reshape x2, local copies, waits for them, and re-layouts, shifted(): return jnp.stack([real, imag], axis=2).reshape(rows, 2 * PAN)  11.1 us
  transfers between devices with their start and end apart: 1, of which 0 were waited for; matrix products, arithmetic and copies ran while one was open for 23% of the time, Pallas kernels for 69%

profile of v1, /device:TPU:7, one launch (start us, length us, event | category | flops | bytes accessed | tf_op | source)
XLA Modules:
  0.0 340.9 jit_solution(8188911012539658844)
XLA Ops:
  0.0 1.9 slice_bitcast_fusion.7
  1.9 0.5 copy-done.2
  2.4 0.2 slice_bitcast_fusion.6
  2.6 0.2 maximum_bitcast_fusion
  2.8 0.2 maximum_bitcast_fusion.2
  3.0 2.4 pad_maximum_fusion.1
  5.4 5.0 %all-to-all-start = ((bf16[4,2,192,1536]{3,2,1,0:T(8,128)(2,1)}), bf16[4,2,192,1536]{3,2,1,0:T(8,128)(2,1)}, u32[]{:S(2)}, u32[]{:S(2)}) async-start(bf16[4,2,192,1536]{3,2,1,0:T(8,128)(2,1)} %pad_maximum_fusion.1), calls=%async_computation | async-start | bytes 9437184 | tf_op jit(solution)/shard_map/all_to_all | solution.py:386
  10.5 0.9 fusion.43
  11.4 0.8 pad_maximum_fusion.3.mine_ref
  12.2 120.8 %shard_map.55 = bf16[4,2,192,384]{3,2,1,0:T(8,128)(2,1)} custom-call(bf16[2,192,384]{2,1,0:T(8,128)(2,1)} %pad_maximum_fusion.3.mine_ref), custom_call_target="tpu_custom_call" | custom-call | bytes 40000000 | tf_op jit(solution)/shard_map/pallas_call | solution.py:96
  133.0 1.4 copy.25
  134.4 0.2 broadcast_in_dim.69.map_ref
  134.6 2.6 constant_dynamic-update-slice_fusion.3
  137.1 89.7 %shard_map.56 = (bf16[2,768,384]{2,1,0:T(8,128)(2,1)}, bf16[2,768,384]{2,1,0:T(8,128)(2,1)}, bf16[2,128,384]{2,1,0:T(8,128)(2,1)}, bf16[2,128,384]{2,1,0:T(8,128)(2,1)}, bf16[2,128,384]{2,1,0:T(8,128)(2,1)}) custom-call(bf16[2,768,384]{2,1,0:T(8,128)(2,1)} %get-tuple-element.46.panel_ref), custom_call_target="tpu_custom_call" | custom-call | bytes 60000000 | tf_op jit(solution)/shard_map/pallas_call | solution.py:186
  226.8 1.6 slice_dynamic-update-slice_fusion.11
  228.4 1.6 slice_dynamic-update-slice_fusion.10
  230.1 1.6 slice_dynamic-update-slice_fusion.9
  231.7 1.6 slice_dynamic-update-slice_fusion.8
  233.3 1.6 slice_dynamic-update-slice_fusion.7
  234.9 1.6 slice_dynamic-update-slice_fusion.6
  236.6 1.6 slice_dynamic-update-slice_fusion.5
  238.2 1.6 slice_dynamic-update-slice_fusion.4
  239.8 1.6 slice_dynamic-update-slice_fusion.3
  241.4 1.6 slice_dynamic-update-slice_fusion.2
  243.1 1.6 slice_dynamic-update-slice_fusion.1
  244.7 1.6 slice_dynamic-update-slice_fusion
  246.3 0.6 fusion.45
  247.5 6.1 %fusion = (f32[1,2304,384]{2,1,0:T(8,128)}, f32[1,2304,384]{2,1,0:T(8,128)}) fusion(bf16[2,2304,384]{2,1,0:T(8,128)(2,1)} %slice_dynamic-update-slice_fusion, f32[]{:T(128)} %bitcast.24, f32[]{:T(128)} %bitcast.26), kind=kLoop, calls=%fused_computation.4 | loop fusion | flops 4423680 | bytes 10616840 | tf_op jit(solution)/shard_map/sub | solution.py:429
  253.6 5.2 %copy.31 = f32[1,2304,384]{1,2,0:T(8,128)} copy(f32[1,2304,384]{2,1,0:T(8,128)} %get-tuple-element.21) | data formatting | bytes 7077888 | tf_op jit(solution)/shard_map/sub | solution.py:429
  258.7 5.2 %copy.32 = f32[1,2304,384]{1,2,0:T(8,128)} copy(f32[1,2304,384]{2,1,0:T(8,128)} %get-tuple-element.22) | data formatting | bytes 7077888 | tf_op jit(solution)/shard_map/mul | solution.py:430
  263.9 0.2 fusion.27
  264.1 0.1 copy.18
  264.2 0.2 fusion.38
  264.4 0.1 copy.19
  264.5 0.2 fusion.46
  264.7 0.2 fusion.41
  264.9 0.1 copy.21
  265.0 0.2 fusion.47
  265.3 0.2 fusion.42
  265.4 0.1 copy.23
  265.6 0.1 pad_add_fusion
  265.6 0.1 add_minimum_fusion
  265.7 0.2 convolution_compare_fusion
  265.9 0.1 broadcast_bitcast_fusion
  266.0 3.7 %broadcast_select_fusion.1 = (f32[2304,3,1,128]{0,3,1,2:T(8,128)S(1)}, f32[2304,3,1,128]{0,3,1,2:T(8,128)S(1)}) fusion(f32[2304,3,1,128]{0,3,1,2:T(8,128)} %bitcast.163, pred[2304,3]{0,1:T(4,128)(4,1)S(1)} %bitcast.169, f32[2304,3,1,128]{0,3,1,2:T(8,128)} %bitcast.164), kind=kLoop, calls=%fused_computation.9 | loop fusion | flops 1769472 | bytes 14162688 | tf_op jit(solution)/shard_map/jit(_where)/select_n | solution.py:429
  269.7 3.4 %pad_maximum_fusion = f32[2304,3,2,128]{0,3,1,2:T(8,128)} fusion(f32[2304,3,1,128]{0,3,1,2:T(8,128)S(1)} %get-tuple-element.40, f32[2304,3,1,128]{0,3,1,2:T(8,128)S(1)} %get-tuple-element.39), kind=kLoop, calls=%fused_computation | loop fusion | flops 1769472 | bytes 14155776 | tf_op jit(solution)/shard_map/stack | solution.py:431
  273.1 12.2 %copy.33 = f32[2304,3,2,128]{3,2,1,0:T(2,128)} copy(f32[2304,3,2,128]{0,3,1,2:T(8,128)} %pad_maximum_fusion) | data formatting | bytes 14155776 | tf_op jit(solution)/shard_map/stack | solution.py:431
  285.4 10.1 %reshape.148.rows_ref = f32[2304,768]{1,0:T(8,128)} reshape(f32[2304,3,2,128]{3,2,1,0:T(2,128)} %copy.33) | data formatting | bytes 14155776 | tf_op jit(solution)/shard_map/reshape | solution.py:431
  295.5 0.2 convolution_compare_fusion.1
  295.7 0.1 copy.24
  295.8 0.1 broadcast_bitcast_fusion.2
  296.0 0.7 fusion.14
  296.8 0.2 copy.28
  297.0 0.2 copy.29
  297.2 0.1 broadcast_select_fusion.3
  297.3 0.1 pad_maximum_fusion.2
  297.4 1.1 copy.30
  298.5 0.9 reshape.147.pivot_ref
  299.6 1.4 copy.43
  301.1 0.2 copy.40
  301.3 1.3 copy-done
  302.5 25.4 %shard_map.57 = (bf16[768,768]{1,0:T(8,128)(2,1)S(1)}, bf16[1536,768]{1,0:T(8,128)(2,1)}, bf16[1536,768]{1,0:T(8,128)(2,1)}) custom-call(f32[384,768]{1,0:T(8,128)S(1)} %reshape.147.pivot_ref, s32[2304,1]{1,0:T(8,128)S(1)} %bitcast.162, f32[2304,768]{1,0:T(8,128)} %reshape.148.rows_ref), custom_call_target="tpu_custom_call" | custom-call | flops 20000000000 | bytes 20000000 | tf_op jit(solution)/shard_map/pallas_call | solution.py:281
  327.9 0.3 fusion.11.keep_ref
  328.2 12.7 %shard_map.58 = f32[2,768,1536]{2,1,0:T(8,128)} custom-call(f32[2]{0:T(128)S(1)} %copy-done.1, f32[6,12]{1,0:T(8,128)S(1)} %fusion.11.keep_ref, bf16[4,2,192,1536]{3,2,1,0:T(8,128)(2,1)} %all-to-all-done.block_ref, s32[768,1]{1,0:T(8,128)S(1)} %broadcast_in_dim.69.map_ref, s32[768,1]{1,0:T(8,128)S(1)} %bitcast.161, ...), custom_call_target="tpu_custom_call" | custom-call | flops 3623878656 | bytes 20000000 | tf_op jit(solution)/shard_map/pallas_call | solution.py:345
  (35 shorter events, 0.6 us)
Async XLA Ops:
  0.0 2.4 copy-start.2
  5.4 322.8 %all-to-all-start = ((bf16[4,2,192,1536]{3,2,1,0:T(8,128)(2,1)}), bf16[4,2,192,1536]{3,2,1,0:T(8,128)(2,1)}, u32[]{:S(2)}, u32[]{:S(2)}) async-start(bf16[4,2,192,1536]{3,2,1,0:T(8,128)(2,1)} %pad_maximum_fusion.1), calls=%async_computation | async-start | bytes 9437184 | tf_op jit(solution)/shard_map/all_to_all | solution.py:386
  10.4 123.9 %copy-start.7 = (s32[768]{0:T(1024)S(1)}, s32[768]{0:T(1024)}, u32[]{:S(2)}) copy-start(s32[768]{0:T(1024)} %param.8) | copy-start | bytes 9220
  137.1 109.2 %copy-start.1 = (f32[2]{0:T(128)S(1)}, f32[2]{0:T(128)}, u32[]{:S(2)}) copy-start(f32[2]{0:T(128)} %shift_ref.1) | copy-start | bytes 28
  258.7 5.2 %copy-start.6 = (s32[48]{0:T(128)S(1)}, s32[48]{0:T(128)}, u32[]{:S(2)}) copy-start(s32[48]{0:T(128)} %param.9) | copy-start | bytes 580
  285.4 10.5 %copy-start.5 = (bf16[2,128,384]{2,1,0:T(8,128)(2,1)S(1)}, bf16[2,128,384]{2,1,0:T(8,128)(2,1)}, u32[]{:S(2)}) copy-start(bf16[2,128,384]{2,1,0:T(8,128)(2,1)} %get-tuple-element.13) | copy-start | bytes 589828
  285.4 10.6 %copy-start.4 = (bf16[2,128,384]{2,1,0:T(8,128)(2,1)S(1)}, bf16[2,128,384]{2,1,0:T(8,128)(2,1)}, u32[]{:S(2)}) copy-start(bf16[2,128,384]{2,1,0:T(8,128)(2,1)} %get-tuple-element.14) | copy-start | bytes 589828
  285.4 10.6 %copy-start.3 = (bf16[2,128,384]{2,1,0:T(8,128)(2,1)S(1)}, bf16[2,128,384]{2,1,0:T(8,128)(2,1)}, u32[]{:S(2)}) copy-start(bf16[2,128,384]{2,1,0:T(8,128)(2,1)} %get-tuple-element.15) | copy-start | bytes 589828
  301.3 1.3 copy-start

commit v2 on v1

--- a/solution.py
+++ b/solution.py
@@ -11,6 +11,7 @@
 STEPS = 3
 NSI = 4
 PAN = STEPS * SN
+PARTS = 4
 VMEM_LIMIT = 50 * 1024 * 1024
 MESH = pl.DeviceIdType.MESH
 
@@ -136,12 +137,16 @@
             copy.start()
             copy.wait()
 
-    def send(i, stage):
+    def view(i, part):
+        height = outs[i].shape[1] // PARTS * 2
+        return outs[i].at[part % 2, pl.ds(part // 2 * height, height)]
+
+    def send(i, part, stage):
         return pltpu.make_async_remote_copy(
-            src_ref=outs[i],
-            dst_ref=outs[i],
-            send_sem=send_sem.at[i, stage],
-            recv_sem=recv_sem.at[i],
+            src_ref=view(i, part),
+            dst_ref=view(i, part),
+            send_sem=send_sem.at[i, part, stage],
+            recv_sem=recv_sem.at[i, part],
             device_id=(pole, partner(orders[i][stage]), col),
             device_id_type=MESH,
         )
@@ -155,26 +160,30 @@
             total = total + relative(i, k)
         return total
 
-    sequence = list(range(groups, items)) + list(range(groups))
+    def arrive(i, part, stage):
+        @pl.when((relative(i, stage) == 1) & (later(i, stage) == 1))
+        def _():
+            send(i, part, stage).wait_recv()
+
+    sequence = [(i, part) for i in range(groups, items) for part in range(PARTS)]
+    sequence += [(i, part) for part in range(PARTS) for i in range(groups)]
     for stage in range(bits):
-        for i in sequence:
+        for i, part in sequence:
+            if stage:
+                arrive(i, part, stage - 1)
 
             @pl.when(later(i, stage) == 0)
             def _():
-                send(i, stage).start()
-
-        for i in sequence:
-
-            @pl.when((relative(i, stage) == 1) & (later(i, stage) == 1))
-            def _():
-                send(i, stage).wait_recv()
-
+                send(i, part, stage).start()
+
+    for i, part in sequence:
+        arrive(i, part, bits - 1)
     for stage in range(bits):
-        for i in sequence:
+        for i, part in sequence:
 
             @pl.when(later(i, stage) == 0)
             def _():
-                send(i, stage).wait_send()
+                send(i, part, stage).wait_send()
 
 
 def tree(panel, n, groups, pcols):
@@ -190,8 +199,8 @@
         out_specs=[pl.BlockSpec(memory_space=pl.ANY)] * items,
         scratch_shapes=[
             pltpu.SemaphoreType.DMA((items,)),
-            pltpu.SemaphoreType.DMA((items, bits)),
-            pltpu.SemaphoreType.DMA((items,)),
+            pltpu.SemaphoreType.DMA((items, PARTS, bits)),
+            pltpu.SemaphoreType.DMA((items, PARTS)),
         ],
         compiler_params=pltpu.CompilerParams(collective_id=1, has_side_effects=True),
         cost_estimate=pl.CostEstimate(flops=0, bytes_accessed=60_000_000, transcendentals=0),
@@ -203,11 +212,30 @@
     return jnp.concatenate([pair, jnp.concatenate([-right, left], axis=1)], axis=0)
 
 
-def panel_kernel(chunk, high, wide, pivot_ref, node_ref, rows_ref, factor_ref, real_ref, imag_ref, inv, step_b, piv):
+def panel_kernel(groups, shift_ref, keep_ref, node_ref, slot_ref, panel_ref, *rest):
+    items = rest[:groups]
+    pivots = rest[groups : groups + STEPS]
+    factor_ref, real_ref, imag_ref, inv, step_b, piv = rest[groups + STEPS :]
     exact = functools.partial(
         jnp.dot, precision=lax.Precision.HIGHEST, preferred_element_type=jnp.float32
     )
-    piv[...] = pivot_ref[...]
+    high = panel_ref.shape[1]
+    wide = real_ref.shape[0]
+    zr, zi = shift_ref[0], shift_ref[1]
+
+    def shifted(ref, span, owner):
+        blocks = []
+        for t in range(STEPS):
+            keep = keep_ref[owner, t] > 0.5
+            ham = ref[0, span, t * SN : (t + 1) * SN].astype(jnp.float32)
+            over = ref[1, span, t * SN : (t + 1) * SN].astype(jnp.float32)
+            pair = jnp.concatenate([ham - zr * over, -zi * over], axis=1)
+            blocks.append(jnp.where(keep, pair, 0.0))
+        return blocks
+
+    for s in range(STEPS):
+        for t, pair in enumerate(shifted(pivots[s], slice(0, SN), s)):
+            piv[s * SN : (s + 1) * SN, 2 * t * SN : 2 * (t + 1) * SN] = pair
     place_r = lax.broadcasted_iota(jnp.int32, (SN, SN), 0)
     place_c = lax.broadcasted_iota(jnp.int32, (SN, SN), 1)
     eye = (place_r == place_c).astype(jnp.float32)
@@ -237,10 +265,9 @@
                 step_b[pairs.index((t, t2))] = link.astype(jnp.bfloat16)
                 piv[below, cols2] = piv[below, cols2] - exact(factor, link)
 
-    def work(start):
-        span = pl.ds(start, chunk)
-        node = node_ref[span, :]
-        blocks = [rows_ref[span, 2 * t * SN : 2 * (t + 1) * SN] for t in range(STEPS)]
+    def work(ref, slot, owner):
+        node = node_ref[owner]
+        blocks = shifted(ref, pl.ds(pl.multiple_of(slot * SN, SN), SN), owner)
         factors = []
         kept = []
         for t in range(STEPS):
@@ -256,37 +283,41 @@
             kept.append(jnp.where(below, blocks[t], 0.0))
         return factors, kept
 
-    @pl.loop(0, high // chunk)
+    @pl.loop(0, high // SN)
     def _(k):
-        start = pl.multiple_of(k * chunk, chunk)
-        factors, kept = work(start)
+        factors, _ = work(panel_ref, k, STEPS + k)
         for t in range(STEPS):
-            factor_ref[pl.ds(start, chunk), 2 * t * SN : 2 * (t + 1) * SN] = factors[t]
-
-    @pl.loop(0, wide // chunk)
-    def _(k):
-        start = pl.multiple_of(k * chunk, chunk)
-        factors, kept = work(pl.multiple_of(high + start, chunk))
-        for t in range(STEPS):
-            re, im = kept[t][:, :SN], kept[t][:, SN:]
-            span = pl.ds(start, chunk)
-            cols = slice(2 * t * SN, 2 * (t + 1) * SN)
-            real_ref[span, cols] = jnp.concatenate([re, -im], axis=1).astype(jnp.bfloat16)
-            imag_ref[span, cols] = jnp.concatenate([im, re], axis=1).astype(jnp.bfloat16)
-
-
-def panels(pivot, nodes, rows, high, wide):
-    chunk = 256
+            span = pl.ds(pl.multiple_of(k * SN, SN), SN)
+            factor_ref[span, 2 * t * SN : 2 * (t + 1) * SN] = factors[t]
+
+    for j in range(groups):
+
+        @pl.loop(0, wide // SN // groups)
+        def _(m):
+            k = m * groups + j
+            _, kept = work(items[j], slot_ref[k], STEPS + high // SN + k)
+            for t in range(STEPS):
+                re, im = kept[t][:, :SN], kept[t][:, SN:]
+                span = pl.ds(pl.multiple_of(k * SN, SN), SN)
+                cols = slice(2 * t * SN, 2 * (t + 1) * SN)
+                real_ref[span, cols] = jnp.concatenate([re, -im], axis=1).astype(jnp.bfloat16)
+                imag_ref[span, cols] = jnp.concatenate([im, re], axis=1).astype(jnp.bfloat16)
+
+
+def panels(shift, keep, owners, slots, panel, spread, groups, wide):
+    high = panel.shape[1]
     bf = jnp.bfloat16
+    smem = pl.BlockSpec(memory_space=pltpu.SMEM)
+    vmem = pl.BlockSpec(memory_space=pltpu.VMEM)
     return pl.pallas_call(
-        functools.partial(panel_kernel, chunk, high, wide),
+        functools.partial(panel_kernel, groups),
         out_shape=[
             jax.ShapeDtypeStruct((high, 2 * PAN), bf),
             jax.ShapeDtypeStruct((wide, 2 * PAN), bf),
             jax.ShapeDtypeStruct((wide, 2 * PAN), bf),
         ],
-        in_specs=[pl.BlockSpec(memory_space=pltpu.VMEM)] * 3,
-        out_specs=[pl.BlockSpec(memory_space=pltpu.VMEM)] * 3,
+        in_specs=[smem] * 4 + [vmem] * (1 + groups + STEPS),
+        out_specs=[vmem] * 3,
         scratch_shapes=[
             pltpu.VMEM((STEPS, 2 * SN, 2 * SN), bf),
             pltpu.VMEM((3, 2 * SN, 2 * SN), bf),
@@ -296,7 +327,7 @@
         cost_estimate=pl.CostEstimate(
             flops=20_000_000_000, bytes_accessed=20_000_000, transcendentals=0
         ),
-    )(pivot, nodes, rows)
+    )(shift, keep, owners, slots, panel, *spread)
 
 
 def update_kernel(tile, shift_ref, keep_ref, block_ref, map_ref, node_ref, factor_ref, real_ref, imag_ref, own_ref, mine_ref, out_ref, pick):
@@ -383,8 +414,6 @@
             for c in range(grid_cols)
         ]
     )
-    block = lax.all_to_all(both, "pcol", split_axis=0, concat_axis=0, tiled=True)
-
     edge = jnp.stack(
         [
             jnp.concatenate([m[:, t * wide : t * wide + SN] for t in range(STEPS)], axis=1)
@@ -392,6 +421,8 @@
         ]
     )
     gathered = line_gather(edge, grid_cols)
+    gathered, both = lax.optimization_barrier((gathered, both))
+    block = lax.all_to_all(both, "pcol", split_axis=0, concat_axis=0, tiled=True)
     gathered = gathered.transpose(1, 0, 2, 3).reshape(2, high, PAN)
     row_places = row_map - my_row * high
     pick = (row_places[:, None] == jnp.arange(high, dtype=jnp.int32)[None, :]).astype(jnp.bfloat16)
@@ -401,15 +432,6 @@
     groups = next(g for g in range(1, grid_rows + 1) if g * grid_cols % grid_rows == 0)
     spread = tree(panel, grid_rows, groups, grid_cols)
 
-    slots = []
-    for k in range(wide // SN):
-        item = spread[k % groups]
-        if grid_rows % grid_cols == 0:
-            slot = k * grid_cols // grid_rows
-            slots.append(item[:, slot * SN : (slot + 1) * SN])
-        else:
-            slot = (k * grid_cols + my_col) // grid_rows
-            slots.append(lax.dynamic_slice_in_dim(item, slot * SN, SN, axis=1))
     pattern = structure(parent, node_count)
     row_nodes = jnp.arange(high // SN, dtype=jnp.int32) * grid_rows + my_row
     col_nodes = jnp.arange(wide // SN, dtype=jnp.int32) * grid_cols + my_col
@@ -418,28 +440,16 @@
     pick_cols = (col_nodes[:, None] == all_nodes[None, :]).astype(jnp.float32)
     keep = jnp.dot(jnp.dot(pick_rows, pattern), pick_cols.T)
 
-    def shifted(raw, owners):
-        rows = raw.shape[1]
-        mask = jnp.dot(
-            (owners[:, None] == all_nodes[None, :]).astype(jnp.float32), pattern[:, :STEPS]
-        )
-        mask = jnp.repeat(mask, SN, axis=0)[:, :, None]
-        ham = raw[0].astype(jnp.float32).reshape(rows, STEPS, SN)
-        over = raw[1].astype(jnp.float32).reshape(rows, STEPS, SN)
-        real = jnp.where(mask > 0.5, ham - pole_shift[0] * over, 0.0)
-        imag = jnp.where(mask > 0.5, -pole_shift[1] * over, 0.0)
-        return jnp.stack([real, imag], axis=2).reshape(rows, 2 * PAN)
-
-    pivot = shifted(jnp.concatenate(spread[groups:], axis=1), all_nodes[:STEPS])
-    owners = jnp.concatenate([row_nodes, col_nodes])
-    rows = shifted(jnp.concatenate([panel] + slots, axis=1), owners)
-    nodes = jnp.repeat(owners, SN)[:, None]
-    factor, real, imag = panels(pivot, nodes, rows, high, wide)
+    owners = jnp.concatenate([all_nodes[:STEPS], row_nodes, col_nodes])
+    slots = col_nodes // grid_rows
+    near = jnp.dot((owners[:, None] == all_nodes[None, :]).astype(jnp.float32), pattern[:, :STEPS])
+    factor, real, imag = panels(pole_shift, near, owners, slots, panel, spread, groups, wide)
+    row_owner = jnp.repeat(row_nodes, SN)[:, None]
     step = jnp.minimum(my_col, STEPS - 1)
     own = lax.dynamic_slice_in_dim(factor, step * 2 * SN, 2 * SN, axis=1)
     mine = jnp.where(my_col < STEPS, my_col, node_count).astype(jnp.int32).reshape(1)
     return update(
-        pole_shift, keep, block, row_places[:, None], nodes[:high], factor, real, imag, own, mine
+        pole_shift, keep, block, row_places[:, None], row_owner, factor, real, imag, own, mine
     )
 
 

time: 342 us -> 179 us (0.52)
  the two profiles are of different devices: /device:TPU:7 before, /device:TPU:0 now
where the time goes in v2:
time: 179 us; the launch traced here: 175 us
  Pallas kernels  153 us (85%)
  local copies, waits for them, and re-layouts  8.34 us (5%)
  other arithmetic  5.18 us (3%)
  starting transfers between devices  5.11 us (3%)
  matrix products  3.75 us (2%)
    pallas_call x1, Pallas kernels, tree(): pl.pallas_call(functools.partial(tree_kernel, n, groups, pcols), out_shap...  75 us
    pallas_call x1, Pallas kernels, line_gather(): pl.pallas_call(functools.partial(line_gather_kernel, n), out_shape=jax.Sh...  36.2 us
    pallas_call x1, Pallas kernels, panels(): pl.pallas_call(functools.partial(panel_kernel, groups), out_shape=[jax.Sh...  29 us
    pallas_call x1, Pallas kernels, update(): pl.pallas_call(functools.partial(update_kernel, tile), grid=(wide // tile...  12.7 us
    all_to_all x1, starting transfers between devices, body(): lax.all_to_all(both, 'pcol', split_axis=0, concat_axis=0, tiled=True)  5.11 us
    another operation x3, other arithmetic, body(): jnp.stack([jnp.stack([m[:, c * wide:(c + 1) * wide] for m in (hamiltonian...  4.16 us
  transfers between devices with their start and end apart: 1, of which 0 were waited for; matrix products, arithmetic and copies ran while one was open for 3% of the time, Pallas kernels for 59%

profile of v2, /device:TPU:0, one launch (start us, length us, event | category | flops | bytes accessed | tf_op | source)
XLA Modules:
  0.0 175.4 jit_solution(14260651359657959963)
XLA Ops:
  0.0 0.9 fusion.40
  0.9 0.0 copy-start.6
  0.9 1.9 %slice_bitcast_fusion.7 = (bf16[1,192,1536]{2,1,0:T(8,128)(2,1)S(1)}, bf16[1,192,1536]{2,1,0:T(8,128)(2,1)S(1)}, bf16[1,192,1536]{2,1,0:T(8,128)(2,1)S(1)}, bf16[1,192,1536]{2,1,0:T(8,128)(2,1)S(1)}) fusion(bf16[192,6144]{1,0:T(8,128)(2,1)} %param.5), kind=kLoop, calls=%fused_computation.20 | loop fusion | bytes 4718592 | tf_op jit(solution)/shard_map/stack | solution.py:413
  2.8 0.5 copy-done.6
  3.3 1.2 slice_bitcast_fusion.6
  4.6 0.7 pad_maximum_fusion.1.mine_ref
  5.3 36.2 %shard_map.55 = bf16[4,2,192,384]{3,2,1,0:T(8,128)(2,1)} custom-call(bf16[2,192,384]{2,1,0:T(8,128)(2,1)} %pad_maximum_fusion.1.mine_ref), custom_call_target="tpu_custom_call" | custom-call | bytes 40000000 | tf_op jit(solution)/shard_map/pallas_call | solution.py:97
  41.5 1.4 maximum_bitcast_fusion
  42.9 0.2 maximum_bitcast_fusion.2
  43.1 2.5 %pad_maximum_fusion = bf16[4,2,192,1536]{3,2,1,0:T(8,128)(2,1)} fusion(bf16[1,2,192,1536]{3,2,1,0:T(8,128)(2,1)S(1)} %get-tuple-element.44, bf16[1,2,192,1536]{3,2,1,0:T(8,128)(2,1)S(1)} %get-tuple-element.43, bf16[1,2,192,1536]{3,2,1,0:T(8,128)(2,1)S(1)} %get-tuple-element.42, bf16[1,2,192,1536]{3,2,1,0:T(8,128)(2,1)S(1)} %get-tuple-element.41), kind=kLoop, calls=%fused_computation | loop fusion | flops 7077888 | bytes 9437184 | tf_op jit(solution)/shard_map/stack | solution.py:411
  45.6 0.0 copy-start.7
  45.6 0.0 copy-start.8
  45.6 5.1 %all-to-all-start = ((bf16[4,2,192,1536]{3,2,1,0:T(8,128)(2,1)}), bf16[4,2,192,1536]{3,2,1,0:T(8,128)(2,1)}, u32[]{:S(2)}, u32[]{:S(2)}) async-start(bf16[4,2,192,1536]{3,2,1,0:T(8,128)(2,1)} %pad_maximum_fusion), calls=%async_computation | async-start | bytes 9437184 | tf_op jit(solution)/shard_map/all_to_all | solution.py:425
  50.8 0.0 copy-start.5
  50.8 0.1 broadcast_bitcast_fusion
  50.9 0.0 copy-done.7
  50.9 0.2 fusion.25
  51.0 0.1 copy.14
  51.1 0.2 fusion.36
  51.3 0.1 copy.15
  51.4 0.2 fusion.42
  51.6 0.1 copy.16
  51.7 0.2 fusion.38
  51.8 0.1 copy.17
  52.0 0.2 fusion.43
  52.1 0.1 copy.18
  52.2 0.2 fusion.39
  52.4 0.1 copy.19
  52.5 0.2 copy.30
  52.7 0.0 copy-done.8
  52.7 0.2 broadcast_in_dim.6.map_ref
  52.9 0.0 copy-done.5
  52.9 0.1 copy.20
  53.0 2.2 %fusion.6.panel_ref = bf16[2,768,384]{2,1,0:T(8,128)(2,1)} fusion(bf16[2,768,384]{2,1,0:T(8,128)(2,1)S(1)} %bitcast.134, s32[768]{0:T(1024)S(1)} %broadcast_subtract_fusion), kind=kOutput, calls=%fused_computation.5 | convolution fusion | flops 907149312 | bytes 2362368 | tf_op jit(solution)/shard_map/nm,pmk->pnk/dot_general | solution.py:429
  55.2 0.0 copy-start
  55.2 0.0 copy-start.1
  55.2 75.0 %shard_map.56 = (bf16[2,768,384]{2,1,0:T(8,128)(2,1)}, bf16[2,768,384]{2,1,0:T(8,128)(2,1)}, bf16[2,128,384]{2,1,0:T(8,128)(2,1)}, bf16[2,128,384]{2,1,0:T(8,128)(2,1)}, bf16[2,128,384]{2,1,0:T(8,128)(2,1)}) custom-call(bf16[2,768,384]{2,1,0:T(8,128)(2,1)} %fusion.6.panel_ref), custom_call_target="tpu_custom_call" | custom-call | bytes 60000000 | tf_op jit(solution)/shard_map/pallas_call | solution.py:195
  130.2 0.1 pad_add_fusion.node_ref
  130.3 0.1 add_minimum_fusion
  130.4 0.2 fusion.30.keep_ref
  130.6 0.0 copy-done
  130.6 0.0 copy-done.1
  130.6 0.0 copy-start.2
  130.6 0.9 copy-done.2
  131.5 0.0 copy-start.3
  131.5 0.9 copy-done.3
  132.5 0.0 copy-start.4
  132.5 0.9 copy-done.4
  133.4 29.0 %shard_map.57 = (bf16[768,768]{1,0:T(8,128)(2,1)S(1)}, bf16[1536,768]{1,0:T(8,128)(2,1)}, bf16[1536,768]{1,0:T(8,128)(2,1)}) custom-call(f32[2]{0:T(128)S(1)} %copy-done.1, f32[21,3]{1,0:T(8,128)S(1)} %fusion.30.keep_ref, s32[21]{0:T(128)S(1)} %pad_add_fusion.node_ref, s32[12]{0:T(128)S(1)} %and_select_fusion.slot_ref, bf16[2,768,384]{2,1,0:T(8,128)(2,1)S(1)} %copy-done, ...), custom_call_target="tpu_custom_call" | custom-call | flops 20000000000 | bytes 20000000 | tf_op jit(solution)/shard_map/pallas_call | solution.py:312
  162.4 0.3 fusion.10.keep_ref
  162.7 0.0 all-to-all-done.block_ref
  162.7 12.7 %shard_map.58 = f32[2,768,1536]{2,1,0:T(8,128)} custom-call(f32[2]{0:T(128)S(1)} %copy-done.1, f32[6,12]{1,0:T(8,128)S(1)} %fusion.10.keep_ref, bf16[4,2,192,1536]{3,2,1,0:T(8,128)(2,1)} %all-to-all-done.block_ref, s32[768,1]{1,0:T(8,128)S(1)} %broadcast_in_dim.6.map_ref, s32[768,1]{1,0:T(8,128)S(1)} %bitcast.132, ...), custom_call_target="tpu_custom_call" | custom-call | flops 3623878656 | bytes 20000000 | tf_op jit(solution)/shard_map/pallas_call | solution.py:376
  (11 shorter events, 0.2 us)
Async XLA Ops:
  0.9 2.4 %copy-start.6 = (bf16[192,6144]{1,0:T(8,128)(2,1)S(1)}, bf16[192,6144]{1,0:T(8,128)(2,1)}, u32[]{:S(2)}) copy-start(bf16[192,6144]{1,0:T(8,128)(2,1)} %param.6) | copy-start | bytes 7077892
  45.6 5.2 %copy-start.7 = (s32[48]{0:T(128)S(1)}, s32[48]{0:T(128)}, u32[]{:S(2)}) copy-start(s32[48]{0:T(128)} %param.9) | copy-start | bytes 580
  45.6 7.0 %copy-start.8 = (s32[768]{0:T(1024)S(1)}, s32[768]{0:T(1024)}, u32[]{:S(2)}) copy-start(s32[768]{0:T(1024)} %param.8) | copy-start | bytes 9220
  45.6 117.1 %all-to-all-start = ((bf16[4,2,192,1536]{3,2,1,0:T(8,128)(2,1)}), bf16[4,2,192,1536]{3,2,1,0:T(8,128)(2,1)}, u32[]{:S(2)}, u32[]{:S(2)}) async-start(bf16[4,2,192,1536]{3,2,1,0:T(8,128)(2,1)} %pad_maximum_fusion), calls=%async_computation | async-start | bytes 9437184 | tf_op jit(solution)/shard_map/all_to_all | solution.py:425
  50.8 2.1 %copy-start.5 = (bf16[4,2,192,384]{3,2,1,0:T(8,128)(2,1)S(1)}, bf16[4,2,192,384]{3,2,1,0:T(8,128)(2,1)}, u32[]{:S(2)}) copy-start(bf16[4,2,192,384]{3,2,1,0:T(8,128)(2,1)} %shard_map.55) | copy-start | bytes 3538948
  55.2 75.4 %copy-start = (bf16[2,768,384]{2,1,0:T(8,128)(2,1)S(1)}, bf16[2,768,384]{2,1,0:T(8,128)(2,1)}, u32[]{:S(2)}) copy-start(bf16[2,768,384]{2,1,0:T(8,128)(2,1)} %fusion.6.panel_ref) | copy-start | bytes 3538948
  55.2 75.4 %copy-start.1 = (f32[2]{0:T(128)S(1)}, f32[2]{0:T(128)}, u32[]{:S(2)}) copy-start(f32[2]{0:T(128)} %shift_ref.3) | copy-start | bytes 28
  130.6 0.9 copy-start.2
  131.5 0.9 copy-start.3
  132.5 0.9 copy-start.4

commit v3 on v2

--- a/solution.py
+++ b/solution.py
@@ -27,70 +27,36 @@
     return jnp.minimum(same + reached + reached.T, 1.0)
 
 
-def line_gather_kernel(n, mine_ref, out_ref, local_sem, up_sem, down_sem, recv_sem):
+def line_gather_kernel(n, mine_ref, out_ref, local_sem, send_sem, recv_sem):
     me = lax.axis_index("pcol")
     row = lax.axis_index("prow")
     pole = lax.axis_index("pole")
     barrier = pltpu.get_barrier_semaphore()
-
-    @pl.when(me + 1 < n)
-    def _():
-        pl.semaphore_signal(barrier, inc=1, device_id=(pole, row, me + 1), device_id_type=MESH)
-
-    @pl.when(me >= 1)
-    def _():
-        pl.semaphore_signal(barrier, inc=1, device_id=(pole, row, me - 1), device_id_type=MESH)
-
-    pl.semaphore_wait(barrier, jnp.where(me + 1 < n, 1, 0) + jnp.where(me >= 1, 1, 0))
-
-    local = pltpu.make_async_copy(mine_ref, out_ref.at[me], local_sem)
-    local.start()
-    local.wait()
-
-    def send(slot, target, sems):
+    for d in range(1, n):
+        pl.semaphore_signal(
+            barrier, inc=1, device_id=(pole, row, (me + d) % n), device_id_type=MESH
+        )
+    pl.semaphore_wait(barrier, n - 1)
+
+    def send(slot, target, d):
         return pltpu.make_async_remote_copy(
-            src_ref=out_ref.at[slot],
+            src_ref=mine_ref,
             dst_ref=out_ref.at[slot],
-            send_sem=sems.at[slot],
+            send_sem=send_sem.at[d],
             recv_sem=recv_sem.at[slot],
             device_id=(pole, row, target),
             device_id_type=MESH,
         )
 
-    for step in range(n):
-        low = me - step
-        high = me + step
-        if step:
-
-            @pl.when(low >= 0)
-            def _():
-                send(low, me, up_sem).wait_recv()
-
-        @pl.when((low >= 0) & (me + 1 < n))
-        def _():
-            send(low, me + 1, up_sem).start()
-
-        if step:
-
-            @pl.when(high < n)
-            def _():
-                send(high, me, down_sem).wait_recv()
-
-        @pl.when((high < n) & (me >= 1))
-        def _():
-            send(high, me - 1, down_sem).start()
-
-    for step in range(n):
-        low = me - step
-        high = me + step
-
-        @pl.when((low >= 0) & (me + 1 < n))
-        def _():
-            send(low, me + 1, up_sem).wait_send()
-
-        @pl.when((high < n) & (me >= 1))
-        def _():
-            send(high, me - 1, down_sem).wait_send()
+    for d in range(1, n):
+        send(me, (me + d) % n, d).start()
+    local = pltpu.make_async_copy(mine_ref, out_ref.at[me], local_sem)
+    local.start()
+    for d in range(1, n):
+        send((me + d) % n, (me + d) % n, d).wait_recv()
+    for d in range(1, n):
+        send(me, (me + d) % n, d).wait_send()
+    local.wait()
 
 
 def line_gather(mine, n):
@@ -101,7 +67,6 @@
         out_specs=pl.BlockSpec(memory_space=pl.ANY),
         scratch_shapes=[
             pltpu.SemaphoreType.DMA,
-            pltpu.SemaphoreType.DMA((n,)),
             pltpu.SemaphoreType.DMA((n,)),
             pltpu.SemaphoreType.DMA((n,)),
         ],
@@ -127,24 +92,16 @@
     roots = [(col + j * pcols) % n for j in range(groups)] + list(range(STEPS))
     forward = list(range(1, bits)) + [0]
     backward = list(range(bits - 1, 0, -1)) + [0]
-    orders = [backward if i % 2 else forward for i in range(items)]
-    for i in range(items):
-
-        @pl.when(me == roots[i])
-        def _():
-            source = panel_ref if i < groups else panel_ref.at[:, 0:SN]
-            copy = pltpu.make_async_copy(source, outs[i], local_sem.at[i])
-            copy.start()
-            copy.wait()
-
-    def view(i, part):
+    orders = [backward if i == groups + 1 else forward for i in range(items)]
+
+    def view(ref, i, part):
         height = outs[i].shape[1] // PARTS * 2
-        return outs[i].at[part % 2, pl.ds(part // 2 * height, height)]
-
-    def send(i, part, stage):
+        return ref.at[part % 2, pl.ds(part // 2 * height, height)]
+
+    def send(i, part, stage, source):
         return pltpu.make_async_remote_copy(
-            src_ref=view(i, part),
-            dst_ref=view(i, part),
+            src_ref=view(source, i, part),
+            dst_ref=view(outs[i], i, part),
             send_sem=send_sem.at[i, part, stage],
             recv_sem=recv_sem.at[i, part],
             device_id=(pole, partner(orders[i][stage]), col),
@@ -163,7 +120,7 @@
     def arrive(i, part, stage):
         @pl.when((relative(i, stage) == 1) & (later(i, stage) == 1))
         def _():
-            send(i, part, stage).wait_recv()
+            send(i, part, stage, outs[i]).wait_recv()
 
     sequence = [(i, part) for i in range(groups, items) for part in range(PARTS)]
     sequence += [(i, part) for part in range(PARTS) for i in range(groups)]
@@ -172,9 +129,25 @@
             if stage:
                 arrive(i, part, stage - 1)
 
-            @pl.when(later(i, stage) == 0)
+            @pl.when(me == roots[i])
             def _():
-                send(i, part, stage).start()
+                send(i, part, stage, panel_ref).start()
+
+            if stage:
+
+                @pl.when((later(i, stage) == 0) & (later(i, 0) > 0))
+                def _():
+                    send(i, part, stage, outs[i]).start()
+
+    def local(i):
+        source = panel_ref if i < groups else panel_ref.at[:, pl.ds(0, SN)]
+        return pltpu.make_async_copy(source, outs[i], local_sem.at[i])
+
+    for i in range(items):
+
+        @pl.when(me == roots[i])
+        def _():
+            local(i).start()
 
     for i, part in sequence:
         arrive(i, part, bits - 1)
@@ -183,7 +156,13 @@
 
             @pl.when(later(i, stage) == 0)
             def _():
-                send(i, part, stage).wait_send()
+                send(i, part, stage, outs[i]).wait_send()
+
+    for i in range(items):
+
+        @pl.when(me == roots[i])
+        def _():
+            local(i).wait()
 
 
 def tree(panel, n, groups, pcols):
@@ -219,6 +198,14 @@
     exact = functools.partial(
         jnp.dot, precision=lax.Precision.HIGHEST, preferred_element_type=jnp.float32
     )
+
+    def fast(left, right):
+        return jnp.dot(
+            left.astype(jnp.bfloat16),
+            right.astype(jnp.bfloat16),
+            preferred_element_type=jnp.float32,
+        )
+
     high = panel_ref.shape[1]
     wide = real_ref.shape[0]
     zr, zi = shift_ref[0], shift_ref[1]
@@ -254,7 +241,8 @@
             jnp.concatenate([eye * (diag_r / modulus), eye * (-diag_i / modulus)], axis=1)
         )
         for sweep in range(NSI):
-            approx = exact(approx, two - exact(full, approx))
+            product = exact if sweep == NSI - 1 else fast
+            approx = product(approx, two - product(full, approx))
         inv[t] = approx.astype(jnp.bfloat16)
         if t + 1 < STEPS:
             below = slice((t + 1) * SN, STEPS * SN)

time: 179 us -> 162 us (0.905); the launches traced: 175 us -> 161 us
  Pallas kernels: 153 us -> 122 us
  waiting for transfers between devices: 0.01 us -> 11.9 us
  starting transfers between devices: 5.11 us -> 10.1 us
    pallas_call x1, Pallas kernels: 75 us -> 61.1 us  [tree(): pl.pallas_call(functools.partial(tree_kernel, n, groups, pcols), out_shap...]
    all_to_all x1, waiting for transfers between devices: 0.01 us -> 11.9 us  [body(): lax.all_to_all(both, 'pcol', split_axis=0, concat_axis=0, tiled=True)]
    pallas_call x1, Pallas kernels: 36.2 us -> 25.4 us  [line_gather(): pl.pallas_call(functools.partial(line_gather_kernel, n), out_shape=jax.Sh...]
    pallas_call x1, Pallas kernels: 29 us -> 22.7 us  [panels(): pl.pallas_call(functools.partial(panel_kernel, groups), out_shape=[jax.Sh...]
    all_to_all x1, starting transfers between devices: 5.11 us -> 10.1 us  [body(): lax.all_to_all(both, 'pcol', split_axis=0, concat_axis=0, tiled=True)]
  transfers between devices with their start and end apart: 1 -> 1, of which waited for: 0 -> 1; matrix products, arithmetic and copies ran while one was open for 3% -> 3% of each run, Pallas kernels for 59% -> 52%
where the time goes in v3:
time: 162 us; the launch traced here: 161 us
  Pallas kernels  122 us (75%)
  waiting for transfers between devices  11.9 us (7%)
  starting transfers between devices  10.1 us (6%)
  local copies, waits for them, and re-layouts  8.34 us (5%)
  other arithmetic  5.18 us (3%)
  matrix products  3.75 us (2%)
    pallas_call x1, Pallas kernels, tree(): pl.pallas_call(functools.partial(tree_kernel, n, groups, pcols), out_shap...  61.1 us
    pallas_call x1, Pallas kernels, line_gather(): pl.pallas_call(functools.partial(line_gather_kernel, n), out_shape=jax.Sh...  25.4 us
    pallas_call x1, Pallas kernels, panels(): pl.pallas_call(functools.partial(panel_kernel, groups), out_shape=[jax.Sh...  22.7 us
    pallas_call x1, Pallas kernels, update(): pl.pallas_call(functools.partial(update_kernel, tile), grid=(wide // tile...  12.7 us
    all_to_all x1, waiting for transfers between devices, body(): lax.all_to_all(both, 'pcol', split_axis=0, concat_axis=0, tiled=True)  11.9 us
    all_to_all x1, starting transfers between devices, body(): lax.all_to_all(both, 'pcol', split_axis=0, concat_axis=0, tiled=True)  10.1 us
    another operation x3, other arithmetic, body(): jnp.stack([jnp.stack([m[:, c * wide:(c + 1) * wide] for m in (hamiltonian...  4.16 us
    unnamed x21, local copies, waits for them, and re-layouts  3.54 us
  transfers between devices with their start and end apart: 1, of which 1 were waited for; matrix products, arithmetic and copies ran while one was open for 3% of the time, Pallas kernels for 52%

profile of v3, /device:TPU:0, one launch (start us, length us, event | category | flops | bytes accessed | tf_op | source)
XLA Modules:
  0.0 161.2 jit_solution(4719972719293897635)
XLA Ops:
  0.0 0.9 fusion.40
  0.9 0.0 copy-start.6
  0.9 1.9 %slice_bitcast_fusion.7 = (bf16[1,192,1536]{2,1,0:T(8,128)(2,1)S(1)}, bf16[1,192,1536]{2,1,0:T(8,128)(2,1)S(1)}, bf16[1,192,1536]{2,1,0:T(8,128)(2,1)S(1)}, bf16[1,192,1536]{2,1,0:T(8,128)(2,1)S(1)}) fusion(bf16[192,6144]{1,0:T(8,128)(2,1)} %param.5), kind=kLoop, calls=%fused_computation.20 | loop fusion | bytes 4718592 | tf_op jit(solution)/shard_map/stack | solution.py:401
  2.8 0.5 copy-done.6
  3.3 1.2 slice_bitcast_fusion.6
  4.6 0.7 pad_maximum_fusion.1.mine_ref
  5.3 25.4 %shard_map.55 = bf16[4,2,192,384]{3,2,1,0:T(8,128)(2,1)} custom-call(bf16[2,192,384]{2,1,0:T(8,128)(2,1)} %pad_maximum_fusion.1.mine_ref), custom_call_target="tpu_custom_call" | custom-call | bytes 40000000 | tf_op jit(solution)/shard_map/pallas_call | solution.py:63
  30.7 1.4 maximum_bitcast_fusion
  32.2 0.2 maximum_bitcast_fusion.2
  32.4 2.5 %pad_maximum_fusion = bf16[4,2,192,1536]{3,2,1,0:T(8,128)(2,1)} fusion(bf16[1,2,192,1536]{3,2,1,0:T(8,128)(2,1)S(1)} %get-tuple-element.44, bf16[1,2,192,1536]{3,2,1,0:T(8,128)(2,1)S(1)} %get-tuple-element.43, bf16[1,2,192,1536]{3,2,1,0:T(8,128)(2,1)S(1)} %get-tuple-element.42, bf16[1,2,192,1536]{3,2,1,0:T(8,128)(2,1)S(1)} %get-tuple-element.41), kind=kLoop, calls=%fused_computation | loop fusion | flops 7077888 | bytes 9437184 | tf_op jit(solution)/shard_map/stack | solution.py:399
  34.9 0.0 copy-start.7
  34.9 0.0 copy-start.8
  34.9 10.1 %all-to-all-start = ((bf16[4,2,192,1536]{3,2,1,0:T(8,128)(2,1)}), bf16[4,2,192,1536]{3,2,1,0:T(8,128)(2,1)}, u32[]{:S(2)}, u32[]{:S(2)}) async-start(bf16[4,2,192,1536]{3,2,1,0:T(8,128)(2,1)} %pad_maximum_fusion), calls=%async_computation | async-start | bytes 9437184 | tf_op jit(solution)/shard_map/all_to_all | solution.py:413
  44.9 0.0 copy-start.5
  44.9 0.1 broadcast_bitcast_fusion
  45.0 0.0 copy-done.7
  45.0 0.2 fusion.25
  45.2 0.1 copy.14
  45.3 0.2 fusion.36
  45.5 0.1 copy.15
  45.6 0.2 fusion.42
  45.7 0.1 copy.16
  45.8 0.2 fusion.38
  46.0 0.1 copy.17
  46.1 0.2 fusion.43
  46.3 0.1 copy.18
  46.4 0.2 fusion.39
  46.5 0.1 copy.19
  46.6 0.2 copy.30
  46.8 0.0 copy-done.8
  46.9 0.2 broadcast_in_dim.6.map_ref
  47.0 0.0 copy-done.5
  47.0 0.1 copy.20
  47.2 2.2 %fusion.6.panel_ref = bf16[2,768,384]{2,1,0:T(8,128)(2,1)} fusion(bf16[2,768,384]{2,1,0:T(8,128)(2,1)S(1)} %bitcast.134, s32[768]{0:T(1024)S(1)} %broadcast_subtract_fusion), kind=kOutput, calls=%fused_computation.5 | convolution fusion | flops 907149312 | bytes 2362368 | tf_op jit(solution)/shard_map/nm,pmk->pnk/dot_general | solution.py:417
  49.4 0.0 copy-start
  49.4 0.0 copy-start.1
  49.4 61.1 %shard_map.56 = (bf16[2,768,384]{2,1,0:T(8,128)(2,1)}, bf16[2,768,384]{2,1,0:T(8,128)(2,1)}, bf16[2,128,384]{2,1,0:T(8,128)(2,1)}, bf16[2,128,384]{2,1,0:T(8,128)(2,1)}, bf16[2,128,384]{2,1,0:T(8,128)(2,1)}) custom-call(bf16[2,768,384]{2,1,0:T(8,128)(2,1)} %fusion.6.panel_ref), custom_call_target="tpu_custom_call" | custom-call | bytes 60000000 | tf_op jit(solution)/shard_map/pallas_call | solution.py:174
  110.5 0.1 pad_add_fusion.node_ref
  110.6 0.1 add_minimum_fusion
  110.7 0.2 fusion.30.keep_ref
  110.9 0.0 copy-done
  110.9 0.0 copy-done.1
  110.9 0.0 copy-start.2
  110.9 0.9 copy-done.2
  111.8 0.0 copy-start.3
  111.8 0.9 copy-done.3
  112.7 0.0 copy-start.4
  112.7 0.9 copy-done.4
  113.7 22.7 %shard_map.57 = (bf16[768,768]{1,0:T(8,128)(2,1)S(1)}, bf16[1536,768]{1,0:T(8,128)(2,1)}, bf16[1536,768]{1,0:T(8,128)(2,1)}) custom-call(f32[2]{0:T(128)S(1)} %copy-done.1, f32[21,3]{1,0:T(8,128)S(1)} %fusion.30.keep_ref, s32[21]{0:T(128)S(1)} %pad_add_fusion.node_ref, s32[12]{0:T(128)S(1)} %and_select_fusion.slot_ref, bf16[2,768,384]{2,1,0:T(8,128)(2,1)S(1)} %copy-done, ...), custom_call_target="tpu_custom_call" | custom-call | flops 20000000000 | bytes 20000000 | tf_op jit(solution)/shard_map/pallas_call | solution.py:300
  136.4 0.3 fusion.10.keep_ref
  136.7 11.9 %all-to-all-done.block_ref = bf16[4,2,192,1536]{3,2,1,0:T(8,128)(2,1)} async-done(((bf16[4,2,192,1536]{3,2,1,0:T(8,128)(2,1)}), bf16[4,2,192,1536]{3,2,1,0:T(8,128)(2,1)}, u32[]{:S(2)}, u32[]{:S(2)}) %all-to-all-start) | async-done | bytes 4718624 | tf_op jit(solution)/shard_map/all_to_all | solution.py:413
  148.5 12.7 %shard_map.58 = f32[2,768,1536]{2,1,0:T(8,128)} custom-call(f32[2]{0:T(128)S(1)} %copy-done.1, f32[6,12]{1,0:T(8,128)S(1)} %fusion.10.keep_ref, bf16[4,2,192,1536]{3,2,1,0:T(8,128)(2,1)} %all-to-all-done.block_ref, s32[768,1]{1,0:T(8,128)S(1)} %broadcast_in_dim.6.map_ref, s32[768,1]{1,0:T(8,128)S(1)} %bitcast.132, ...), custom_call_target="tpu_custom_call" | custom-call | flops 3623878656 | bytes 20000000 | tf_op jit(solution)/shard_map/pallas_call | solution.py:364
  (11 shorter events, 0.2 us)
Async XLA Ops:
  0.9 2.4 %copy-start.6 = (bf16[192,6144]{1,0:T(8,128)(2,1)S(1)}, bf16[192,6144]{1,0:T(8,128)(2,1)}, u32[]{:S(2)}) copy-start(bf16[192,6144]{1,0:T(8,128)(2,1)} %param.6) | copy-start | bytes 7077892
  34.9 10.2 %copy-start.7 = (s32[48]{0:T(128)S(1)}, s32[48]{0:T(128)}, u32[]{:S(2)}) copy-start(s32[48]{0:T(128)} %param.9) | copy-start | bytes 580
  34.9 12.0 %copy-start.8 = (s32[768]{0:T(1024)S(1)}, s32[768]{0:T(1024)}, u32[]{:S(2)}) copy-start(s32[768]{0:T(1024)} %param.8) | copy-start | bytes 9220
  34.9 113.7 %all-to-all-start = ((bf16[4,2,192,1536]{3,2,1,0:T(8,128)(2,1)}), bf16[4,2,192,1536]{3,2,1,0:T(8,128)(2,1)}, u32[]{:S(2)}, u32[]{:S(2)}) async-start(bf16[4,2,192,1536]{3,2,1,0:T(8,128)(2,1)} %pad_maximum_fusion), calls=%async_computation | async-start | bytes 9437184 | tf_op jit(solution)/shard_map/all_to_all | solution.py:413
  44.9 2.1 %copy-start.5 = (bf16[4,2,192,384]{3,2,1,0:T(8,128)(2,1)S(1)}, bf16[4,2,192,384]{3,2,1,0:T(8,128)(2,1)}, u32[]{:S(2)}) copy-start(bf16[4,2,192,384]{3,2,1,0:T(8,128)(2,1)} %shard_map.55) | copy-start | bytes 3538948
  49.4 61.5 %copy-start = (bf16[2,768,384]{2,1,0:T(8,128)(2,1)S(1)}, bf16[2,768,384]{2,1,0:T(8,128)(2,1)}, u32[]{:S(2)}) copy-start(bf16[2,768,384]{2,1,0:T(8,128)(2,1)} %fusion.6.panel_ref) | copy-start | bytes 3538948
  49.4 61.5 %copy-start.1 = (f32[2]{0:T(128)S(1)}, f32[2]{0:T(128)}, u32[]{:S(2)}) copy-start(f32[2]{0:T(128)} %shift_ref.3) | copy-start | bytes 28
  110.9 0.9 copy-start.2
  111.8 0.9 copy-start.3
  112.7 0.9 copy-start.4

commit v4 on v3

--- a/solution.py
+++ b/solution.py
@@ -27,68 +27,97 @@
     return jnp.minimum(same + reached + reached.T, 1.0)
 
 
-def line_gather_kernel(n, mine_ref, out_ref, local_sem, send_sem, recv_sem):
-    me = lax.axis_index("pcol")
-    row = lax.axis_index("prow")
-    pole = lax.axis_index("pole")
-    barrier = pltpu.get_barrier_semaphore()
-    for d in range(1, n):
-        pl.semaphore_signal(
-            barrier, inc=1, device_id=(pole, row, (me + d) % n), device_id_type=MESH
-        )
-    pl.semaphore_wait(barrier, n - 1)
-
-    def send(slot, target, d):
-        return pltpu.make_async_remote_copy(
-            src_ref=mine_ref,
-            dst_ref=out_ref.at[slot],
-            send_sem=send_sem.at[d],
-            recv_sem=recv_sem.at[slot],
-            device_id=(pole, row, target),
-            device_id_type=MESH,
-        )
-
-    for d in range(1, n):
-        send(me, (me + d) % n, d).start()
-    local = pltpu.make_async_copy(mine_ref, out_ref.at[me], local_sem)
-    local.start()
-    for d in range(1, n):
-        send((me + d) % n, (me + d) % n, d).wait_recv()
-    for d in range(1, n):
-        send(me, (me + d) % n, d).wait_send()
-    local.wait()
-
-
-def line_gather(mine, n):
-    return pl.pallas_call(
-        functools.partial(line_gather_kernel, n),
-        out_shape=jax.ShapeDtypeStruct((n,) + mine.shape, mine.dtype),
-        in_specs=[pl.BlockSpec(memory_space=pl.ANY)],
-        out_specs=pl.BlockSpec(memory_space=pl.ANY),
-        scratch_shapes=[
-            pltpu.SemaphoreType.DMA,
-            pltpu.SemaphoreType.DMA((n,)),
-            pltpu.SemaphoreType.DMA((n,)),
-        ],
-        compiler_params=pltpu.CompilerParams(collective_id=0, has_side_effects=True),
-        cost_estimate=pl.CostEstimate(flops=0, bytes_accessed=40_000_000, transcendentals=0),
-    )(mine)
-
-
-def tree_kernel(n, groups, pcols, panel_ref, *rest):
+def real_form(pair):
+    left, right = pair[:, :SN], pair[:, SN:]
+    return jnp.concatenate([pair, jnp.concatenate([-right, left], axis=1)], axis=0)
+
+
+def move_kernel(
+    n, pcols, groups, shift_ref, keep_ref, map_ref, ham_ref, over_ref,
+    block_ref, factor_ref, real_ref, imag_ref,
+    edges, pick, panel, inv, step_b, piv, *rest
+):
     items = groups + STEPS
     outs = rest[:items]
-    local_sem, send_sem, recv_sem = rest[items:]
+    edge_sem, line_send, line_recv, own_sem, block_send, block_recv = rest[items : items + 6]
+    local_sem, send_sem, recv_sem = rest[items + 6 :]
     me = lax.axis_index("prow")
     col = lax.axis_index("pcol")
     pole = lax.axis_index("pole")
+    wide = block_ref.shape[3]
+    high = panel.shape[1]
+    sources = (ham_ref, over_ref)
     bits = n.bit_length() - 1
     bit = lambda value, b: (value // (1 << b)) % 2
     partner = lambda b: me + (1 << b) * (1 - 2 * bit(me, b))
     barrier = pltpu.get_barrier_semaphore()
+
+    def edge(a, t):
+        return pltpu.make_async_copy(
+            sources[a].at[:, pl.ds(t * wide, SN)],
+            edges.at[col, a, :, pl.ds(t * SN, SN)],
+            edge_sem.at[a, t],
+        )
+
+    for a in range(2):
+        for t in range(STEPS):
+            edge(a, t).start()
+    for d in range(1, pcols):
+        pl.semaphore_signal(
+            barrier, inc=1, device_id=(pole, me, (col + d) % pcols), device_id_type=MESH
+        )
     for b in range(bits):
         pl.semaphore_signal(barrier, inc=1, device_id=(pole, partner(b), col), device_id_type=MESH)
-    pl.semaphore_wait(barrier, bits)
+    for a in range(2):
+        for t in range(STEPS):
+            edge(a, t).wait()
+    pl.semaphore_wait(barrier, pcols - 1 + bits)
+
+    def line(slot, target, d):
+        return pltpu.make_async_remote_copy(
+            src_ref=edges.at[slot],
+            dst_ref=edges.at[slot],
+            send_sem=line_send.at[d],
+            recv_sem=line_recv.at[slot],
+            device_id=(pole, me, target),
+            device_id_type=MESH,
+        )
+
+    def block(a, column, slot, target, d):
+        return pltpu.make_async_remote_copy(
+            src_ref=sources[a].at[:, pl.ds(pl.multiple_of(column * wide, SN), wide)],
+            dst_ref=block_ref.at[slot, a],
+            send_sem=block_send.at[a, d],
+            recv_sem=block_recv.at[a, slot],
+            device_id=(pole, me, target),
+            device_id_type=MESH,
+        )
+
+    def own(a):
+        return pltpu.make_async_copy(
+            sources[a].at[:, pl.ds(pl.multiple_of(col * wide, SN), wide)],
+            block_ref.at[col, a],
+            own_sem.at[a],
+        )
+
+    for d in range(1, pcols):
+        line(col, (col + d) % pcols, d).start()
+    place = lax.broadcasted_iota(jnp.int32, (high, high), 1)
+    pick[...] = (place == map_ref[...]).astype(jnp.bfloat16)
+    for d in range(1, pcols):
+        line(col, (col + d) % pcols, d).wait_send()
+    for d in range(1, pcols):
+        for a in range(2):
+            block(a, (col + d) % pcols, col, (col + d) % pcols, d).start()
+    for a in range(2):
+        own(a).start()
+    for d in range(1, pcols):
+        line((col + d) % pcols, (col + d) % pcols, d).wait_recv()
+    for a in range(2):
+        panel[a] = jnp.dot(
+            pick[...], edges[:, a].reshape(high, PAN), preferred_element_type=jnp.float32
+        ).astype(jnp.bfloat16)
+
     roots = [(col + j * pcols) % n for j in range(groups)] + list(range(STEPS))
     forward = list(range(1, bits)) + [0]
     backward = list(range(bits - 1, 0, -1)) + [0]
@@ -131,7 +160,7 @@
 
             @pl.when(me == roots[i])
             def _():
-                send(i, part, stage, panel_ref).start()
+                send(i, part, stage, panel).start()
 
             if stage:
 
@@ -140,7 +169,7 @@
                     send(i, part, stage, outs[i]).start()
 
     def local(i):
-        source = panel_ref if i < groups else panel_ref.at[:, pl.ds(0, SN)]
+        source = panel if i < groups else panel.at[:, pl.ds(0, SN)]
         return pltpu.make_async_copy(source, outs[i], local_sem.at[i])
 
     for i in range(items):
@@ -164,37 +193,6 @@
         def _():
             local(i).wait()
 
-
-def tree(panel, n, groups, pcols):
-    bits = n.bit_length() - 1
-    items = groups + STEPS
-    shapes = [jax.ShapeDtypeStruct(panel.shape, panel.dtype)] * groups + [
-        jax.ShapeDtypeStruct((2, SN, PAN), panel.dtype)
-    ] * STEPS
-    return pl.pallas_call(
-        functools.partial(tree_kernel, n, groups, pcols),
-        out_shape=shapes,
-        in_specs=[pl.BlockSpec(memory_space=pl.ANY)],
-        out_specs=[pl.BlockSpec(memory_space=pl.ANY)] * items,
-        scratch_shapes=[
-            pltpu.SemaphoreType.DMA((items,)),
-            pltpu.SemaphoreType.DMA((items, PARTS, bits)),
-            pltpu.SemaphoreType.DMA((items, PARTS)),
-        ],
-        compiler_params=pltpu.CompilerParams(collective_id=1, has_side_effects=True),
-        cost_estimate=pl.CostEstimate(flops=0, bytes_accessed=60_000_000, transcendentals=0),
-    )(panel)
-
-
-def real_form(pair):
-    left, right = pair[:, :SN], pair[:, SN:]
-    return jnp.concatenate([pair, jnp.concatenate([-right, left], axis=1)], axis=0)
-
-
-def panel_kernel(groups, shift_ref, keep_ref, node_ref, slot_ref, panel_ref, *rest):
-    items = rest[:groups]
-    pivots = rest[groups : groups + STEPS]
-    factor_ref, real_ref, imag_ref, inv, step_b, piv = rest[groups + STEPS :]
     exact = functools.partial(
         jnp.dot, precision=lax.Precision.HIGHEST, preferred_element_type=jnp.float32
     )
@@ -206,8 +204,6 @@
             preferred_element_type=jnp.float32,
         )
 
-    high = panel_ref.shape[1]
-    wide = real_ref.shape[0]
     zr, zi = shift_ref[0], shift_ref[1]
 
     def shifted(ref, span, owner):
@@ -221,7 +217,7 @@
         return blocks
 
     for s in range(STEPS):
-        for t, pair in enumerate(shifted(pivots[s], slice(0, SN), s)):
+        for t, pair in enumerate(shifted(outs[groups + s], slice(0, SN), s)):
             piv[s * SN : (s + 1) * SN, 2 * t * SN : 2 * (t + 1) * SN] = pair
     place_r = lax.broadcasted_iota(jnp.int32, (SN, SN), 0)
     place_c = lax.broadcasted_iota(jnp.int32, (SN, SN), 1)
@@ -253,8 +249,7 @@
                 step_b[pairs.index((t, t2))] = link.astype(jnp.bfloat16)
                 piv[below, cols2] = piv[below, cols2] - exact(factor, link)
 
-    def work(ref, slot, owner):
-        node = node_ref[owner]
+    def work(ref, slot, owner, node):
         blocks = shifted(ref, pl.ds(pl.multiple_of(slot * SN, SN), SN), owner)
         factors = []
         kept = []
@@ -273,7 +268,7 @@
 
     @pl.loop(0, high // SN)
     def _(k):
-        factors, _ = work(panel_ref, k, STEPS + k)
+        factors, _ = work(panel, k, STEPS + k, k * n + me)
         for t in range(STEPS):
             span = pl.ds(pl.multiple_of(k * SN, SN), SN)
             factor_ref[span, 2 * t * SN : 2 * (t + 1) * SN] = factors[t]
@@ -283,7 +278,7 @@
         @pl.loop(0, wide // SN // groups)
         def _(m):
             k = m * groups + j
-            _, kept = work(items[j], slot_ref[k], STEPS + high // SN + k)
+            _, kept = work(outs[j], (k * pcols + col) // n, STEPS + high // SN + k, k * pcols + col)
             for t in range(STEPS):
                 re, im = kept[t][:, :SN], kept[t][:, SN:]
                 span = pl.ds(pl.multiple_of(k * SN, SN), SN)
@@ -291,31 +286,62 @@
                 real_ref[span, cols] = jnp.concatenate([re, -im], axis=1).astype(jnp.bfloat16)
                 imag_ref[span, cols] = jnp.concatenate([im, re], axis=1).astype(jnp.bfloat16)
 
-
-def panels(shift, keep, owners, slots, panel, spread, groups, wide):
-    high = panel.shape[1]
+    for a in range(2):
+        for d in range(1, pcols):
+            block(a, (col + d) % pcols, (col + d) % pcols, (col + d) % pcols, d).wait_recv()
+    for a in range(2):
+        for d in range(1, pcols):
+            block(a, (col + d) % pcols, col, (col + d) % pcols, d).wait_send()
+    for a in range(2):
+        own(a).wait()
+
+
+def move(shift, keep, row_places, hamiltonian, margin, n, pcols, groups):
+    high = row_places.shape[0]
+    share, total = hamiltonian.shape
+    wide = total // pcols
+    bits = n.bit_length() - 1
+    items = groups + STEPS
     bf = jnp.bfloat16
     smem = pl.BlockSpec(memory_space=pltpu.SMEM)
     vmem = pl.BlockSpec(memory_space=pltpu.VMEM)
+    hbm = pl.BlockSpec(memory_space=pl.ANY)
+    dma = pltpu.SemaphoreType.DMA
     return pl.pallas_call(
-        functools.partial(panel_kernel, groups),
+        functools.partial(move_kernel, n, pcols, groups),
         out_shape=[
+            jax.ShapeDtypeStruct((pcols, 2, share, wide), bf),
             jax.ShapeDtypeStruct((high, 2 * PAN), bf),
             jax.ShapeDtypeStruct((wide, 2 * PAN), bf),
             jax.ShapeDtypeStruct((wide, 2 * PAN), bf),
         ],
-        in_specs=[smem] * 4 + [vmem] * (1 + groups + STEPS),
-        out_specs=[vmem] * 3,
+        in_specs=[smem, smem, vmem, hbm, hbm],
+        out_specs=[hbm, vmem, vmem, vmem],
         scratch_shapes=[
+            pltpu.VMEM((pcols, 2, share, PAN), bf),
+            pltpu.VMEM((high, high), bf),
+            pltpu.VMEM((2, high, PAN), bf),
             pltpu.VMEM((STEPS, 2 * SN, 2 * SN), bf),
             pltpu.VMEM((3, 2 * SN, 2 * SN), bf),
             pltpu.VMEM((PAN, 2 * PAN), jnp.float32),
+        ]
+        + [pltpu.VMEM((2, high, PAN), bf)] * groups
+        + [pltpu.VMEM((2, SN, PAN), bf)] * STEPS
+        + [
+            dma((2, STEPS)),
+            dma((pcols,)),
+            dma((pcols,)),
+            dma((2,)),
+            dma((2, pcols)),
+            dma((2, pcols)),
+            dma((items,)),
+            dma((items, PARTS, bits)),
+            dma((items, PARTS)),
         ],
-        compiler_params=pltpu.CompilerParams(vmem_limit_bytes=VMEM_LIMIT),
-        cost_estimate=pl.CostEstimate(
-            flops=20_000_000_000, bytes_accessed=20_000_000, transcendentals=0
+        compiler_params=pltpu.CompilerParams(
+            collective_id=0, has_side_effects=True, vmem_limit_bytes=VMEM_LIMIT
         ),
-    )(shift, keep, owners, slots, panel, *spread)
+    )(shift, keep, row_places, hamiltonian, margin)
 
 
 def update_kernel(tile, shift_ref, keep_ref, block_ref, map_ref, node_ref, factor_ref, real_ref, imag_ref, own_ref, mine_ref, out_ref, pick):
@@ -396,30 +422,8 @@
     high = row_map.shape[0]
     node_count = parent.shape[0]
 
-    both = jnp.stack(
-        [
-            jnp.stack([m[:, c * wide : (c + 1) * wide] for m in (hamiltonian, margin)])
-            for c in range(grid_cols)
-        ]
-    )
-    edge = jnp.stack(
-        [
-            jnp.concatenate([m[:, t * wide : t * wide + SN] for t in range(STEPS)], axis=1)
-            for m in (hamiltonian, margin)
-        ]
-    )
-    gathered = line_gather(edge, grid_cols)
-    gathered, both = lax.optimization_barrier((gathered, both))
-    block = lax.all_to_all(both, "pcol", split_axis=0, concat_axis=0, tiled=True)
-    gathered = gathered.transpose(1, 0, 2, 3).reshape(2, high, PAN)
     row_places = row_map - my_row * high
-    pick = (row_places[:, None] == jnp.arange(high, dtype=jnp.int32)[None, :]).astype(jnp.bfloat16)
-    panel = jnp.einsum("nm,pmk->pnk", pick, gathered, preferred_element_type=jnp.float32).astype(
-        jnp.bfloat16
-    )
     groups = next(g for g in range(1, grid_rows + 1) if g * grid_cols % grid_rows == 0)
-    spread = tree(panel, grid_rows, groups, grid_cols)
-
     pattern = structure(parent, node_count)
     row_nodes = jnp.arange(high // SN, dtype=jnp.int32) * grid_rows + my_row
     col_nodes = jnp.arange(wide // SN, dtype=jnp.int32) * grid_cols + my_col
@@ -429,9 +433,10 @@
     keep = jnp.dot(jnp.dot(pick_rows, pattern), pick_cols.T)
 
     owners = jnp.concatenate([all_nodes[:STEPS], row_nodes, col_nodes])
-    slots = col_nodes // grid_rows
     near = jnp.dot((owners[:, None] == all_nodes[None, :]).astype(jnp.float32), pattern[:, :STEPS])
-    factor, real, imag = panels(pole_shift, near, owners, slots, panel, spread, groups, wide)
+    block, factor, real, imag = move(
+        pole_shift, near, row_places[:, None], hamiltonian, margin, grid_rows, grid_cols, groups
+    )
     row_owner = jnp.repeat(row_nodes, SN)[:, None]
     step = jnp.minimum(my_col, STEPS - 1)
     own = lax.dynamic_slice_in_dim(factor, step * 2 * SN, 2 * SN, axis=1)

time: 162 us -> 175 us (1.080)
  the two profiles are of different devices: /device:TPU:0 before, /device:TPU:27 now
where the time goes in v4:
time: 175 us; the launch traced here: 174 us
  Pallas kernels  166 us (95%)
  local copies, waits for them, and re-layouts  3.03 us (2%)
  matrix products  3 us (2%)
  other arithmetic  2.25 us (1%)
    pallas_call x1, Pallas kernels, move(): pl.pallas_call(functools.partial(move_kernel, n, pcols, groups), out_shap...  153 us
    pallas_call x1, Pallas kernels, update(): pl.pallas_call(functools.partial(update_kernel, tile), grid=(wide // tile...  12.7 us

profile of v4, /device:TPU:27, one launch (start us, length us, event | category | flops | bytes accessed | tf_op | source)
XLA Modules:
  0.0 174.3 jit_solution(16501376680988102076)
XLA Ops:
  0.0 0.1 pad_add_fusion
  0.1 0.7 broadcast_subtract_fusion
  0.8 0.1 broadcast_bitcast_fusion
  0.9 0.9 fusion.15
  1.8 0.1 copy.13
  1.8 0.9 fusion.26
  2.8 0.1 copy.14
  2.8 0.7 minimum_convert_fusion.4
  3.5 0.2 fusion.30
  3.7 0.1 copy.15
  3.8 0.2 fusion.28
  4.0 0.1 copy.16
  4.1 0.2 fusion.31
  4.2 0.1 copy.17
  4.3 0.2 fusion.29
  4.5 0.1 copy.18
  4.6 0.8 add_minimum_fusion
  5.3 0.3 fusion.keep_ref
  5.6 0.2 fusion.20.keep_ref
  5.8 0.2 broadcast_in_dim.6.map_ref
  6.0 0.2 copy.25
  6.2 0.0 copy-start.1
  6.2 0.7 copy-done.1
  6.8 153.3 %shard_map.55 = (bf16[4,2,192,1536]{3,2,1,0:T(8,128)(2,1)}, bf16[768,768]{1,0:T(8,128)(2,1)S(1)}, bf16[1536,768]{1,0:T(8,128)(2,1)S(1)}, bf16[1536,768]{1,0:T(8,128)(2,1)}) custom-call(f32[2]{0:T(128)S(1)} %copy-done.1, f32[21,3]{1,0:T(8,128)S(1)} %fusion.20.keep_ref, s32[768,1]{1,0:T(8,128)S(1)} %broadcast_in_dim.6.map_ref, bf16[192,6144]{1,0:T(8,128)(2,1)} %ham_ref.1, ...), custom_call_target="tpu_custom_call" | custom-call | tf_op jit(solution)/shard_map/pallas_call | solution.py:310
  160.1 0.0 copy-start
  160.1 1.5 copy-done
  161.6 12.7 %shard_map.56 = f32[2,768,1536]{2,1,0:T(8,128)} custom-call(f32[2]{0:T(128)S(1)} %copy-done.1, f32[6,12]{1,0:T(8,128)S(1)} %fusion.keep_ref, bf16[4,2,192,1536]{3,2,1,0:T(8,128)(2,1)} %get-tuple-element.9.block_ref, s32[768,1]{1,0:T(8,128)S(1)} %broadcast_in_dim.6.map_ref, s32[768,1]{1,0:T(8,128)S(1)} %bitcast.92, ...), custom_call_target="tpu_custom_call" | custom-call | flops 3623878656 | bytes 20000000 | tf_op jit(solution)/shard_map/pallas_call | solution.py:390
  (6 shorter events, 0.1 us)
Async XLA Ops:
  6.2 0.7 copy-start.1
  160.1 1.5 copy-start

commit v5 on v4

--- a/solution.py
+++ b/solution.py
@@ -93,6 +93,13 @@
             device_id_type=MESH,
         )
 
+    def far(d):
+        down = pcols - d
+        down = down - jnp.where(down <= col, 1, 0)
+        up = d - 1
+        up = up + jnp.where(up >= col, 1, 0)
+        return jnp.where(col < pcols // 2, down, up)
+
     def own(a):
         return pltpu.make_async_copy(
             sources[a].at[:, pl.ds(pl.multiple_of(col * wide, SN), wide)],
@@ -108,7 +115,7 @@
         line(col, (col + d) % pcols, d).wait_send()
     for d in range(1, pcols):
         for a in range(2):
-            block(a, (col + d) % pcols, col, (col + d) % pcols, d).start()
+            block(a, far(d), col, far(d), d).start()
     for a in range(2):
         own(a).start()
     for d in range(1, pcols):
@@ -291,7 +298,7 @@
             block(a, (col + d) % pcols, (col + d) % pcols, (col + d) % pcols, d).wait_recv()
     for a in range(2):
         for d in range(1, pcols):
-            block(a, (col + d) % pcols, col, (col + d) % pcols, d).wait_send()
+            block(a, far(d), col, far(d), d).wait_send()
     for a in range(2):
         own(a).wait()
 

time: 175 us -> 157 us (0.90)
  the two profiles are of different devices: /device:TPU:27 before, /device:TPU:0 now
where the time goes in v5:
time: 157 us; the launch traced here: 156 us
  Pallas kernels  148 us (94%)
  local copies, waits for them, and re-layouts  3.03 us (2%)
  matrix products  3 us (2%)
  other arithmetic  2.25 us (1%)
    pallas_call x1, Pallas kernels, move(): pl.pallas_call(functools.partial(move_kernel, n, pcols, groups), out_shap...  135 us
    pallas_call x1, Pallas kernels, update(): pl.pallas_call(functools.partial(update_kernel, tile), grid=(wide // tile...  12.7 us

profile of v5, /device:TPU:0, one launch (start us, length us, event | category | flops | bytes accessed | tf_op | source)
XLA Modules:
  0.0 156.4 jit_solution(11938209316060153750)
XLA Ops:
  0.0 0.1 pad_add_fusion
  0.1 0.7 broadcast_subtract_fusion
  0.8 0.1 broadcast_bitcast_fusion
  0.9 0.9 fusion.15
  1.8 0.1 copy.13
  1.8 0.9 fusion.26
  2.8 0.1 copy.14
  2.8 0.7 minimum_convert_fusion.4
  3.5 0.2 fusion.30
  3.7 0.1 copy.15
  3.8 0.2 fusion.28
  3.9 0.1 copy.16
  4.1 0.2 fusion.31
  4.2 0.1 copy.17
  4.3 0.2 fusion.29
  4.5 0.1 copy.18
  4.6 0.8 add_minimum_fusion
  5.3 0.3 fusion.keep_ref
  5.6 0.2 fusion.20.keep_ref
  5.8 0.2 broadcast_in_dim.6.map_ref
  6.0 0.2 copy.25
  6.2 0.0 copy-start.1
  6.2 0.7 copy-done.1
  6.8 135.4 %shard_map.55 = (bf16[4,2,192,1536]{3,2,1,0:T(8,128)(2,1)}, bf16[768,768]{1,0:T(8,128)(2,1)S(1)}, bf16[1536,768]{1,0:T(8,128)(2,1)S(1)}, bf16[1536,768]{1,0:T(8,128)(2,1)}) custom-call(f32[2]{0:T(128)S(1)} %copy-done.1, f32[21,3]{1,0:T(8,128)S(1)} %fusion.20.keep_ref, s32[768,1]{1,0:T(8,128)S(1)} %broadcast_in_dim.6.map_ref, bf16[192,6144]{1,0:T(8,128)(2,1)} %ham_ref.1, ...), custom_call_target="tpu_custom_call" | custom-call | tf_op jit(solution)/shard_map/pallas_call | solution.py:317
  142.2 0.0 copy-start
  142.2 1.5 copy-done
  143.7 12.7 %shard_map.56 = f32[2,768,1536]{2,1,0:T(8,128)} custom-call(f32[2]{0:T(128)S(1)} %copy-done.1, f32[6,12]{1,0:T(8,128)S(1)} %fusion.keep_ref, bf16[4,2,192,1536]{3,2,1,0:T(8,128)(2,1)} %get-tuple-element.9.block_ref, s32[768,1]{1,0:T(8,128)S(1)} %broadcast_in_dim.6.map_ref, s32[768,1]{1,0:T(8,128)S(1)} %bitcast.92, ...), custom_call_target="tpu_custom_call" | custom-call | flops 3623878656 | bytes 20000000 | tf_op jit(solution)/shard_map/pallas_call | solution.py:397
  (6 shorter events, 0.1 us)
Async XLA Ops:
  6.2 0.7 copy-start.1
  142.2 1.5 copy-start
